TPU v7x, 256 devices: a whole 4x4x8 slice. The times are simulated.
256 devices in a mesh: ctx: 16 (over z_hi, x), dp: 16 (over z_lo, y, core).
Axes of the slice: x: 4, y: 4, z: 8 (z_hi: 4, z_lo: 2; z = z_hi * 2 + z_lo), core: 2. Of those that a mesh axis runs over, the one named last changes fastest.
Arguments:
- doc_states: bfloat16 [4096, 4096], P('dp', 'ctx'), may hold values from -3 to 3
- context: bfloat16 [128, 4096], P('ctx'), may hold values from -6 to 6
- norm_gain: float32 [4096], replicated, may hold values from 0.5 to 1.5
- w_query: bfloat16 [4096, 2048], P(None, 'ctx'), may hold values from -0.09375 to 0.09375
- w_key: bfloat16 [4096, 2048], P(None, 'ctx'), may hold values from -0.09375 to 0.09375
- w_value: bfloat16 [4096, 2048], P(None, 'ctx'), may hold values from -0.09375 to 0.09375
- w_out: bfloat16 [2048, 4096], P('ctx'), may hold values from -0.125 to 0.125
- partners: int32 [64], P('dp'), may hold values from 0 to 63, as said below
Outputs:
- loss: float32 [], replicated
- grad_context: float32 [128, 4096], P('ctx')
- grad_query: float32 [4096, 2048], P('dp', 'ctx')
- grad_key: float32 [4096, 2048], P('dp', 'ctx')
- grad_value: float32 [4096, 2048], P('dp', 'ctx')
- grad_out: float32 [2048, 4096], P('ctx', 'dp')
Inputs may be any that keep to these rules, and one draw needn't show every extreme that they name: partners[i] != i, and every document is the partner of exactly one document.
All inputs are finite; a program needn't handle non-finite values.
Results may differ from a plain program's by a relative error of at most 0.017.
Values may be sent and summed in bfloat16 or wider, within the bound.
No kernel may reach another device: no remote copies, remote signals or barrier semaphores. Data moves between devices by JAX's collectives and lax.ppermute only.
A program may use at most 64 MiB of HBM per device.

v0:
```python
import jax
import jax.numpy as jnp
from jax import lax
from jax.sharding import PartitionSpec as P

HD = 128
DOC_LEN = 64


epsilon = 1e-05
sharpness_divisor = 0.05
loss_scale = 65536.0
exact_arithmetic_setting = lax.Precision.HIGHEST


def to_wide(array):
    return array.astype(jnp.float32)


def rms_norm(matrix, gain_row):
    widened = to_wide(matrix)
    inverse_rms = lax.rsqrt(jnp.mean(widened * widened, axis=-1, keepdims=True) + epsilon)
    return ((widened * inverse_rms * gain_row).astype(jnp.bfloat16), inverse_rms)


def narrow_product(form, left, right):
    return jnp.einsum(form, left, right, preferred_element_type=jnp.float32)


def attend(queries, doc_keys, doc_values, ctx_keys, ctx_values):
    factor = queries.shape[-1] ** (-0.5)
    ctx_scores = narrow_product("blhe,che->bhlc", queries, ctx_keys) * factor
    own_scores = narrow_product("blhe,bmhe->bhlm", queries, doc_keys) * factor
    ctx_exps = jnp.exp(ctx_scores)
    own_exps = jnp.exp(own_scores)
    normalizer = jnp.sum(ctx_exps, axis=-1, keepdims=True) + jnp.sum(
        own_exps, axis=-1, keepdims=True
    )
    ctx_probs = ctx_exps / normalizer
    own_probs = own_exps / normalizer
    ctx_weights = ctx_probs.astype(jnp.bfloat16)
    own_weights = own_probs.astype(jnp.bfloat16)
    mixture = narrow_product("bhlc,che->blhe", ctx_weights, ctx_values)
    mixture = mixture + narrow_product("bhlm,bmhe->blhe", own_weights, doc_values)
    return (mixture.astype(jnp.bfloat16), (ctx_probs, own_probs, ctx_weights, own_weights))


def attend_back(grad_mixture, queries, doc_keys, doc_values, ctx_keys, ctx_values, saved):
    ctx_probs, own_probs, ctx_weights, own_weights = saved
    factor = queries.shape[-1] ** (-0.5)
    ctx_dweights = narrow_product("blhe,che->bhlc", grad_mixture, ctx_values)
    own_dweights = narrow_product("blhe,bmhe->bhlm", grad_mixture, doc_values)
    inner_sum = jnp.sum(ctx_probs * ctx_dweights, axis=-1, keepdims=True) + jnp.sum(
        own_probs * own_dweights, axis=-1, keepdims=True
    )
    ctx_dscores = (ctx_probs * (ctx_dweights - inner_sum) * factor).astype(jnp.bfloat16)
    own_dscores = (own_probs * (own_dweights - inner_sum) * factor).astype(jnp.bfloat16)
    grad_queries = narrow_product("bhlc,che->blhe", ctx_dscores, ctx_keys)
    grad_queries = grad_queries + narrow_product("bhlm,bmhe->blhe", own_dscores, doc_keys)
    grad_keys = narrow_product("bhlm,blhe->bmhe", own_dscores, queries)
    grad_values = narrow_product("bhlm,blhe->bmhe", own_weights, grad_mixture)
    grad_ctx_keys = narrow_product("bhlc,blhe->che", ctx_dscores, queries)
    grad_ctx_values = narrow_product("bhlc,blhe->che", ctx_weights, grad_mixture)
    return (
        grad_queries.astype(jnp.bfloat16),
        grad_keys.astype(jnp.bfloat16),
        grad_values.astype(jnp.bfloat16),
        grad_ctx_keys,
        grad_ctx_values,
    )


def project(matrix, weight):
    return jnp.dot(matrix, weight, preferred_element_type=jnp.float32).astype(jnp.bfloat16)


def shards(doc_states, context, norm_gain, w_query, w_key, w_value, w_out, partners):
    tok_rows = doc_states.shape[0]
    local_docs = tok_rows // DOC_LEN
    head_count = w_query.shape[1] // HD
    local_width = head_count * HD
    full_rows = lax.all_gather(doc_states, "ctx", axis=1, tiled=True)
    normed, doc_inverse = rms_norm(full_rows, norm_gain)
    queries = project(normed, w_query).reshape(local_docs, DOC_LEN, head_count, HD)
    doc_keys = project(normed, w_key).reshape(local_docs, DOC_LEN, head_count, HD)
    doc_values = project(normed, w_value).reshape(local_docs, DOC_LEN, head_count, HD)
    context_all = lax.all_gather(context, "ctx", axis=0, tiled=True)
    ctx_count = context_all.shape[0]
    ctx_normed, ctx_all_inverse = rms_norm(context_all, norm_gain)
    ctx_keys = project(ctx_normed, w_key).reshape(ctx_count, head_count, HD)
    ctx_values = project(ctx_normed, w_value).reshape(ctx_count, head_count, HD)
    mixture, saved = attend(queries, doc_keys, doc_values, ctx_keys, ctx_values)
    mixture_rows = mixture.reshape(tok_rows, local_width)
    own_mean = jnp.mean(to_wide(doc_states).reshape(local_docs, DOC_LEN, -1), axis=1)
    branch = jnp.dot(mixture_rows, w_out, preferred_element_type=jnp.float32)
    branch = lax.psum_scatter(branch, "ctx", scatter_dimension=1, tiled=True)
    pooled = own_mean + jnp.mean(branch.reshape(local_docs, DOC_LEN, -1), axis=1)
    everyone = lax.all_gather(pooled, "dp", axis=0, tiled=True)
    doc_total = everyone.shape[0]
    gram_part = jnp.dot(pooled, everyone.T, precision=exact_arithmetic_setting)
    square_part = jnp.sum(everyone * everyone, axis=1)
    cosine_affinity_grid, squares = lax.psum((gram_part, square_part), "ctx")
    euclidean_magnitude = jnp.sqrt(squares + 1e-06)
    first_doc = lax.axis_index("dp") * local_docs
    local_vector_length = lax.dynamic_slice_in_dim(euclidean_magnitude, first_doc, local_docs)
    raw_affinity_table = (
        cosine_affinity_grid
        / (local_vector_length[:, None] * euclidean_magnitude[None, :])
        / sharpness_divisor
    )
    doc_ids = jnp.arange(doc_total, dtype=jnp.int32)
    own_ids = first_doc + jnp.arange(local_docs, dtype=jnp.int32)
    others = own_ids[:, None] != doc_ids[None, :]
    exp_scores = jnp.where(others, jnp.exp(raw_affinity_table), 0.0)
    row_totals = jnp.sum(exp_scores, axis=1)
    chosen = (partners[:, None] == doc_ids[None, :]).astype(jnp.float32)
    picked = jnp.sum(raw_affinity_table * chosen, axis=1)
    loss_part = jnp.sum(jnp.log(row_totals) - picked)
    loss = lax.psum(loss_part, "dp") / doc_total
    couple_weighting = (exp_scores / row_totals[:, None] - chosen) / doc_total * loss_scale
    gathered_unit_vectors = everyone / euclidean_magnitude[:, None]
    unit_mine = pooled / local_vector_length[:, None]
    column_gradient_term = jnp.dot(
        couple_weighting.T, unit_mine, precision=exact_arithmetic_setting
    )
    column_gradient_term = lax.psum_scatter(
        column_gradient_term, "dp", scatter_dimension=0, tiled=True
    )
    direction_loss_slope = (
        jnp.dot(couple_weighting, gathered_unit_vectors, precision=exact_arithmetic_setting)
        + column_gradient_term
    ) / sharpness_divisor
    radial = lax.psum(jnp.sum(unit_mine * direction_loss_slope, axis=1), "ctx")
    grad_pooled = (direction_loss_slope - unit_mine * radial[:, None]) / local_vector_length[
        :, None
    ]
    out_wide = to_wide(w_out)
    per_token = jnp.broadcast_to(
        (grad_pooled / DOC_LEN)[:, None, :], (local_docs, DOC_LEN, grad_pooled.shape[1])
    )
    per_token = lax.all_gather(per_token.reshape(tok_rows, -1), "ctx", axis=1, tiled=True)
    grad_rows = jnp.dot(per_token, out_wide.T, precision=exact_arithmetic_setting).astype(
        jnp.bfloat16
    )
    grad_out_part = jnp.dot(to_wide(mixture_rows).T, per_token, precision=exact_arithmetic_setting)
    grad_out = lax.psum_scatter(grad_out_part, "dp", scatter_dimension=1, tiled=True)
    grad_mixture = grad_rows.reshape(local_docs, DOC_LEN, head_count, HD)
    grad_queries, grad_keys, grad_values, grad_ctx_keys, grad_ctx_values = attend_back(
        grad_mixture, queries, doc_keys, doc_values, ctx_keys, ctx_values, saved
    )
    query_rows = grad_queries.reshape(tok_rows, local_width)
    key_rows = grad_keys.reshape(tok_rows, local_width)
    value_rows = grad_values.reshape(tok_rows, local_width)
    ctx_key_rows = grad_ctx_keys.reshape(ctx_count, local_width)
    ctx_value_rows = grad_ctx_values.reshape(ctx_count, local_width)
    ctx_columns = to_wide(ctx_normed)
    part_query = jnp.dot(normed.T, query_rows, preferred_element_type=jnp.float32)
    part_key = jnp.dot(normed.T, key_rows, preferred_element_type=jnp.float32)
    part_key = part_key + jnp.dot(ctx_columns.T, ctx_key_rows, precision=exact_arithmetic_setting)
    part_value = jnp.dot(normed.T, value_rows, preferred_element_type=jnp.float32)
    part_value = part_value + jnp.dot(
        ctx_columns.T, ctx_value_rows, precision=exact_arithmetic_setting
    )
    stacked = lax.psum_scatter(
        jnp.concatenate([part_query, part_key, part_value], axis=1),
        "dp",
        scatter_dimension=0,
        tiled=True,
    )
    grad_query = stacked[:, :local_width]
    grad_key = stacked[:, local_width : 2 * local_width]
    grad_value = stacked[:, 2 * local_width :]
    key_wide = to_wide(w_key)
    value_wide = to_wide(w_value)
    grad_ctx_normed = jnp.dot(
        ctx_key_rows, key_wide.T, precision=exact_arithmetic_setting
    ) + jnp.dot(ctx_value_rows, value_wide.T, precision=exact_arithmetic_setting)
    grad_ctx_normed = lax.psum(grad_ctx_normed, "dp")
    grad_ctx_normed = lax.psum_scatter(grad_ctx_normed, "ctx", scatter_dimension=0, tiled=True)
    context_wide = to_wide(context)
    ctx_inverse = lax.rsqrt(jnp.mean(context_wide * context_wide, axis=-1, keepdims=True) + epsilon)
    scaled = norm_gain * grad_ctx_normed
    grad_context = ctx_inverse * scaled - context_wide * ctx_inverse**3 * jnp.mean(
        context_wide * scaled, axis=1, keepdims=True
    )
    return (loss, grad_context, grad_query, grad_key, grad_value, grad_out)


def solution(mesh):
    in_specs = (
        P("dp", "ctx"),
        P("ctx", None),
        P(),
        P(None, "ctx"),
        P(None, "ctx"),
        P(None, "ctx"),
        P("ctx", None),
        P("dp"),
    )
    out_specs = (
        P(),
        P("ctx", None),
        P("dp", "ctx"),
        P("dp", "ctx"),
        P("dp", "ctx"),
        P("ctx", "dp"),
    )
    return jax.shard_map(shards, mesh=mesh, in_specs=in_specs, out_specs=out_specs, check_vma=False)
```

profile of v0, /device:TPU:1, one launch (start us, length us, event | category | flops | bytes accessed | tf_op | source)
XLA Modules:
  0.0 896.4 jit_solution(7780771050784099499)
XLA Ops:
  7.2 0.7 all-gather.5.cloned.1.call-update
  8.0 0.7 all-gather.7.cloned.1.call-update
  8.7 57.8 %all-gather.5.cloned.1.call-done = bf16[128,4096]{1,0:T(8,128)(2,1)} async-done(((bf16[8,4096]{1,0:T(8,128)(2,1)}), bf16[128,4096]{1,0:T(8,128)(2,1)}) %all-gather.5.cloned.1.call-update) | async-done | bytes 1048592 | tf_op jit(solution)/shard_map/all_gather | solution.py:87
  66.6 1.6 fusion.3
  68.2 2.1 fusion.14
  70.3 0.5 fusion.13
  70.8 59.4 %all-gather.7.cloned.1.call-done = bf16[256,4096]{1,0:T(8,128)(2,1)} async-done(((bf16[256,256]{1,0:T(8,128)(2,1)}), bf16[256,4096]{1,0:T(8,128)(2,1)}) %all-gather.7.cloned.1.call-update) | async-done | bytes 2097168 | tf_op jit(solution)/shard_map/all_gather | solution.py:82
  130.2 2.2 fusion
  132.5 0.6 fusion.2
  133.1 0.6 copy-done.8
  133.7 0.7 convolution_convert_fusion
  134.4 0.5 copy-done.5
  134.9 0.7 convolution_convert_fusion.1
  135.6 0.5 copy-done.10
  136.1 0.7 convolution_convert_fusion.2
  137.1 0.3 fusion.43
  137.4 0.6 copy-done.13
  138.5 2.6 fusion.45
  141.2 0.8 copy-done.12
  142.1 91.7 %reduce-scatter.5.cloned.1.call-done = f32[256,256]{1,0:T(8,128)} async-done(((f32[256,4096]{1,0:T(8,128)}), f32[256,256]{1,0:T(8,128)}) %reduce-scatter.5.cloned.1.call-update) | async-done | bytes 262160 | tf_op jit(solution)/shard_map/reduce_scatter | solution.py:96
  233.7 1.0 bitcast_reduce_fusion
  234.7 20.2 %all-gather = f32[16,4,256]{2,1,0:T(4,128)S(1)} all-gather(f32[1,4,256]{2,1,0:T(4,128)S(1)} %fusion.33), channel_id=1, replica_groups=mesh['ctx'=16,'dp'=16] {'dp'}, dimensions={0}, use_global_device_ids=true | all-gather | bytes 69632 | tf_op jit(solution)/shard_map/all_gather | solution.py:98
  255.2 35.5 %all-reduce.1 = (f32[4,64]{1,0:T(4,128)S(1)}, f32[64]{0:T(128)S(1)}) all-reduce(f32[4,64]{1,0:T(4,128)S(1)} %fusion.32, f32[64]{0:T(128)S(1)} %multiply_reduce_fusion.2), channel_id=1, replica_groups=mesh['ctx'=16,'dp'=16] {'ctx'}, use_global_device_ids=true, to_apply=%region_7.0 | all-reduce | flops 320 | bytes 2560 | tf_op jit(solution)/shard_map/psum | solution.py:102
  290.9 0.7 fusion.31
  291.7 1.0 fusion.34
  292.7 0.6 dynamic-slice
  293.9 109.3 %all-reduce.7.cloned.1.call-done = f32[64,256]{1,0:T(8,128)} async-done(((f32[64,256]{1,0:T(8,128)}), f32[64,256]{1,0:T(8,128)}) %all-reduce.7.cloned.1.call-update) | async-done | bytes 65552
  403.1 1.0 multiply_reduce_fusion.3
  404.2 37.8 %psum.38 = f32[4]{0:T(128)S(1)} all-reduce(f32[4]{0:T(128)S(1)} %get-tuple-element.34), channel_id=1, replica_groups=mesh['ctx'=16,'dp'=16] {'ctx'}, use_global_device_ids=true, to_apply=%region_17.18 | all-reduce | flops 4 | bytes 32 | tf_op jit(solution)/shard_map/psum | solution.py:133
  442.0 0.7 broadcast_in_dim.6
  442.9 84.6 %all-gather.9.cloned.1.call-done = f32[256,4096]{1,0:T(8,128)} async-done(((f32[256,256]{1,0:T(8,128)}), f32[256,4096]{1,0:T(8,128)}) %all-gather.9.cloned.1.call-update) | async-done | bytes 4194320 | tf_op jit(solution)/shard_map/all_gather | solution.py:141
  527.4 4.2 convolution_convert_fusion.3
  531.6 1.0 convolution_bitcast_fusion.5
  532.7 1.8 multiply_reduce_fusion
  534.4 1.1 multiply_reduce_fusion.1
  535.6 0.6 copy-done.27
  536.2 0.8 fusion.20
  537.2 1.0 fusion.46
  538.2 2.4 convolution_add_fusion.2
  540.9 0.9 convolution_bitcast_fusion.2
  541.9 0.9 multiply_convert_fusion
  542.9 1.0 convolution_convert_fusion.4
  544.2 1.8 fusion.47
  546.0 0.5 fusion.48
  546.5 0.5 fusion.49
  547.0 0.7 copy-done.3
  547.7 2.4 convolution_add_fusion
  550.1 2.5 convolution_add_fusion.1
  552.6 73.6 %reduce-scatter.11.cloned.1.call-done = f32[8,4096]{1,0:T(8,128)} async-done(((f32[128,4096]{1,0:T(8,128)}), f32[8,4096]{1,0:T(8,128)}) %reduce-scatter.11.cloned.1.call-update) | async-done | bytes 131088 | tf_op jit(solution)/shard_map/reduce_scatter | solution.py:179
  626.3 5.6 pad_maximum_fusion
  631.9 0.8 copy-done.19
  632.7 5.2 fusion.50
  637.9 0.6 copy-done.32
  638.5 0.6 subtract_reduce_fusion
  639.1 29.7 %psum.37 = f32[]{:T(128)} all-reduce(f32[]{:T(128)} %subtract_reduce_fusion), channel_id=1, replica_groups=mesh['ctx'=16,'dp'=16] {'dp'}, use_global_device_ids=true, to_apply=%region_13.14 | all-reduce | flops 1 | bytes 8 | tf_op jit(solution)/shard_map/psum | solution.py:119
  669.5 78.7 %all-reduce.5.cloned.1.call-done = f32[8,4096]{1,0:T(8,128)} async-done(((f32[8,4096]{1,0:T(8,128)}), f32[8,4096]{1,0:T(8,128)}) %all-reduce.5.cloned.1.call-update) | async-done | bytes 131088 | tf_op jit(solution)/shard_map/psum | solution.py:178
  748.2 1.1 fusion.16
  749.3 1.7 fusion.18
  750.9 70.5 %reduce-scatter.7.cloned.1.call-done = f32[256,384]{0,1:T(8,128)} async-done(((f32[4096,384]{0,1:T(8,128)}), f32[256,384]{0,1:T(8,128)}) %reduce-scatter.7.cloned.1.call-update) | async-done | bytes 393232 | tf_op jit(solution)/shard_map/reduce_scatter | solution.py:164
  821.4 1.1 fusion.42
  822.5 0.8 copy.23
  823.2 0.8 copy.22
  824.0 0.8 copy.21
  824.7 64.0 %reduce-scatter.9.cloned.1.call-done = f32[128,256]{1,0:T(8,128)} async-done(((f32[128,4096]{1,0:T(8,128)}), f32[128,256]{1,0:T(8,128)}) %reduce-scatter.9.cloned.1.call-update) | async-done | bytes 131088 | tf_op jit(solution)/shard_map/reduce_scatter | solution.py:146
  (101 shorter events, 2.6 us)
Async XLA Ops:
  7.2 131.3 %copy-start = (bf16[128,4096]{1,0:T(8,128)(2,1)S(1)}, bf16[128,4096]{1,0:T(8,128)(2,1)}, u32[]{:S(2)}) copy-start(bf16[128,4096]{1,0:T(8,128)(2,1)} %param.14) | copy-start | bytes 3145732
  7.2 63.1 %copy-start.17 = (f32[4096]{0:T(1024)S(1)}, f32[4096]{0:T(1024)}, u32[]{:S(2)}) copy-start(f32[4096]{0:T(1024)} %param.10) | copy-start | bytes 49156
  7.2 63.1 %copy-start.7 = (bf16[4096,128]{1,0:T(8,128)(2,1)S(1)}, bf16[4096,128]{1,0:T(8,128)(2,1)}, u32[]{:S(2)}) copy-start(bf16[4096,128]{1,0:T(8,128)(2,1)} %param.13) | copy-start | bytes 3145732
  7.2 59.4 %all-gather.5.cloned.1.call-start = ((), (), s32[]{:S(2)}) async-start(), calls=%async_computation.4 | async-start | bytes 1114112 | tf_op jit(solution)/shard_map/all_gather | solution.py:87
  7.9 122.2 %all-gather.7.cloned.1.call-start = ((), (), s32[]{:S(2)}) async-start(), calls=%async_computation.5 | async-start | bytes 2228224 | tf_op jit(solution)/shard_map/all_gather | solution.py:82
  8.7 225.0 %reduce-scatter.5.cloned.1.call-start = ((), (), s32[]{:S(2)}) async-start(), calls=%async_computation.6 | async-start | bytes 4456448 | tf_op jit(solution)/shard_map/reduce_scatter | solution.py:96
  66.6 3.7 copy-start.2
  68.2 2.6 copy-start.28
  70.3 66.7 %copy-start.22 = (bf16[128,128,1]{1,0,2:T(8,128)(2,1)}, bf16[128,128,1]{1,0,2:T(8,128)(2,1)S(1)}, u32[]{:S(2)}) copy-start(bf16[128,128,1]{1,0,2:T(8,128)(2,1)S(1)} %fusion.14) | copy-start | bytes 98308
  70.8 66.6 %copy-start.35 = (bf16[128,128,1]{1,0,2:T(8,128)(2,1)}, bf16[128,128,1]{1,0,2:T(8,128)(2,1)S(1)}, u32[]{:S(2)}) copy-start(bf16[128,128,1]{1,0,2:T(8,128)(2,1)S(1)} %fusion.13) | copy-start | bytes 98308
  130.2 2.2 copy-start.4
  132.4 1.2 copy-start.8
  133.7 1.2 copy-start.5
  134.9 3.3 copy-start.23
  134.9 1.2 copy-start.10
  137.0 1.2 copy-start.15
  137.3 0.7 copy-start.13
  137.4 3.8 copy-start.26
  138.5 2.7 copy-start.18
  141.1 0.9 copy-start.12
  141.1 149.8 %copy-start.30 = (s32[4]{0:T(128)S(1)}, s32[4]{0:T(128)}, u32[]{:S(2)}) copy-start(s32[4]{0:T(128)} %param.15) | copy-start | bytes 52
  141.1 151.6 %copy-start.34 = (u32[256]{0:T(256)S(1)}, u32[256]{0:T(256)}, u32[]{:S(2)}) copy-start(u32[256]{0:T(256)} %constant.51) | copy-start | bytes 3076
  141.2 262.0 %all-reduce.7.cloned.1.call-start = ((), (), s32[]{:S(2)}) async-start(), calls=%async_computation.12 | async-start | bytes 131072
  291.7 151.1 %copy-start.31 = (f32[4]{0:T(128)}, f32[4]{0:T(128)S(1)}, u32[]{:S(2)}) copy-start(f32[4]{0:T(128)S(1)} %get-tuple-element.20) | copy-start | bytes 52
  292.6 234.8 %all-gather.9.cloned.1.call-start = ((), (), s32[]{:S(2)}) async-start(), calls=%async_computation.7 | async-start | bytes 4456448 | tf_op jit(solution)/shard_map/all_gather | solution.py:141
  442.8 88.8 %copy-start.14 = (f32[4,1,64,128]{3,2,0,1:T(8,128)S(1)}, f32[4,1,64,128]{3,2,0,1:T(8,128)}, u32[]{:S(2)}) copy-start(f32[4,1,64,128]{3,2,0,1:T(8,128)} %copy-done.13) | copy-start | bytes 393220
  442.8 89.8 %copy-start.24 = (bf16[256,128]{1,0:T(8,128)(2,1)S(1)}, bf16[256,128]{1,0:T(8,128)(2,1)}, u32[]{:S(2)}) copy-start(bf16[256,128]{1,0:T(8,128)(2,1)} %copy-done.23) | copy-start | bytes 196612
  442.8 183.4 %reduce-scatter.11.cloned.1.call-start = ((), (), s32[]{:S(2)}) async-start(), calls=%async_computation.10 | async-start | bytes 2228224 | tf_op jit(solution)/shard_map/reduce_scatter | solution.py:179
  531.6 3.9 copy-start.25
  531.6 5.5 copy-start.6
  532.7 5.6 copy-start.20
  534.4 3.8 copy-start.9
  535.6 0.6 copy-start.27
  540.7 1.2 copy-start.16
  540.7 207.5 %all-reduce.5.cloned.1.call-start = ((), (), s32[]{:S(2)}) async-start(), calls=%async_computation.11 | async-start | bytes 262144 | tf_op jit(solution)/shard_map/psum | solution.py:178
  546.4 1.2 copy-start.3
  546.5 1.2 copy-start.21
  546.5 1.2 copy-start.29
  550.1 76.2 %copy-start.1 = (f32[4096,128]{0,1:T(8,128)S(1)}, f32[4096,128]{0,1:T(8,128)}, u32[]{:S(2)}) copy-start(f32[4096,128]{0,1:T(8,128)} %fusion.47) | copy-start | bytes 6291460
  626.2 195.2 %reduce-scatter.7.cloned.1.call-start = ((), (), s32[]{:S(2)}) async-start(), calls=%async_computation.8 | async-start | bytes 6684672 | tf_op jit(solution)/shard_map/reduce_scatter | solution.py:164
  631.9 0.8 copy-start.19
  631.9 256.9 %reduce-scatter.9.cloned.1.call-start = ((), (), s32[]{:S(2)}) async-start(), calls=%async_computation.9 | async-start | bytes 2228224 | tf_op jit(solution)/shard_map/reduce_scatter | solution.py:146
  637.9 0.7 copy-start.32
  637.9 0.7 copy-start.33
  637.9 110.3 %copy-start.11 = (bf16[8,4096]{1,0:T(8,128)(2,1)S(1)}, bf16[8,4096]{1,0:T(8,128)(2,1)}, u32[]{:S(2)}) copy-start(bf16[8,4096]{1,0:T(8,128)(2,1)} %param.9) | copy-start | bytes 196612
Sparse Core Ops, SparseCore 0:
  10.5 56.0 all-gather.4
  69.0 61.1 all-gather.6
  141.3 92.3 reduce-scatter.4
  292.8 110.3 all-reduce.6
  442.9 84.4 all-gather.8
  540.8 85.3 reduce-scatter.10
  629.0 119.1 all-reduce.4
  750.7 70.6 reduce-scatter.6
  824.5 64.2 reduce-scatter.8
where the time goes:
time: 900 us; the launch traced here: 896 us
  waiting for transfers between devices  691 us (77%)
  blocking collectives  123 us (14%)
  matrix products  37.1 us (4%)
  other arithmetic  17.2 us (2%)
  between operations  16.7 us (2%)
  local copies, waits for them, and re-layouts  10.6 us (1%)
    unnamed x10, waiting for transfers between devices  111 us
    reduce_scatter x1, waiting for transfers between devices, shards(): branch = lax.psum_scatter(branch, 'ctx', scatter_dimension=1, tiled=True)  91.7 us
    all_gather x1, waiting for transfers between devices, shards(): lax.all_gather(per_token.reshape(tok_rows, -1), 'ctx', axis=1, tiled=True)  84.6 us
    psum x1, waiting for transfers between devices, shards(): grad_ctx_normed = lax.psum(grad_ctx_normed, 'dp')  78.7 us
    reduce_scatter x1, waiting for transfers between devices, shards(): lax.psum_scatter(grad_ctx_normed, 'ctx', scatter_dimension=0, tiled=True)  73.6 us
    reduce_scatter x1, waiting for transfers between devices, shards(): lax.psum_scatter(jnp.concatenate([part_query, part_key, part_value], axis...  70.5 us
    reduce_scatter x1, waiting for transfers between devices, shards(): lax.psum_scatter(grad_out_part, 'dp', scatter_dimension=1, tiled=True)  64 us
    all_gather x1, waiting for transfers between devices, shards(): full_rows = lax.all_gather(doc_states, 'ctx', axis=1, tiled=True)  59.4 us
  transfers between devices with their start and end apart: 9, of which 9 were waited for; matrix products, arithmetic and copies ran while one was open for 4% of the time, Pallas kernels for 0%

commit v1 on v0

v1 whole, which is shorter than its diff:
```python
import jax
import jax.numpy as jnp
from jax import lax
from jax.sharding import Mesh, PartitionSpec as P

HD = 128
DOC_LEN = 64

EPS = 1e-05
TEMPERATURE = 0.05
LOSS_SCALE = 65536.0
EXACT = lax.Precision.HIGHEST

CTX = ("zh", "x")
DP = ("zl", "y", "co")
EVERY = CTX + DP

f32 = jnp.float32
bf16 = jnp.bfloat16


def wide(a):
    return a.astype(f32)


def pieces(a, count):
    out = []
    for _ in range(count):
        head = lax.reduce_precision(a, 8, 7)
        out.append(head.astype(bf16))
        a = a - head
    return out


def dot(a, b):
    return jnp.dot(a, b, preferred_element_type=f32)


def split_dot(a, b, count):
    rows = a.shape[0]
    got = dot(jnp.concatenate(pieces(a, count), axis=0), b)
    return sum(got[i * rows : (i + 1) * rows] for i in reversed(range(count)))


def ein(form, a, b):
    return jnp.einsum(form, a, b, preferred_element_type=f32)


def inverse_rms(a):
    return lax.rsqrt(jnp.mean(a * a, axis=-1, keepdims=True) + EPS)


def spread(block, axis, size):
    copies = jnp.broadcast_to(block[None], (size,) + block.shape)
    return lax.all_to_all(copies, axis, 0, 0)


def probabilities(queries, doc_keys, ctx_keys):
    factor = HD**-0.5
    ctx_exps = jnp.exp(ein("ble,ce->blc", queries, ctx_keys) * factor)
    own_exps = jnp.exp(ein("ble,bme->blm", queries, doc_keys) * factor)
    total = jnp.sum(ctx_exps, -1, keepdims=True) + jnp.sum(own_exps, -1, keepdims=True)
    return ctx_exps / total, own_exps / total


def shards(doc_states, context, gain, w_query, w_key, w_value, w_out, partners):
    n_ctx, n_dp = 16, 16
    tok = doc_states.shape[0]
    feat = doc_states.shape[1]
    docs = tok // DOC_LEN
    width = feat * n_ctx
    swap = [(c * 16 + d, d * 16 + c) for c in range(16) for d in range(16)]
    dp_id = lax.axis_index(DP)
    co_id = lax.axis_index("co")

    own_ctx = wide(context)
    own_ctx_inv = inverse_rms(own_ctx)
    own_ctx_normed = (own_ctx * own_ctx_inv * gain).astype(bf16)
    ctx_normed = lax.all_gather(lax.ppermute(own_ctx_normed, EVERY, swap), DP, axis=0, tiled=True)
    columns = lax.all_gather(lax.ppermute(doc_states, EVERY, swap), CTX, axis=0, tiled=True)

    by_zh = lax.all_gather(doc_states, "zh")
    rows = wide(spread(by_zh, "x", 4).transpose(2, 1, 0, 3).reshape(tok, width))
    doc_inv = inverse_rms(rows)
    normed = (rows * doc_inv * gain).astype(bf16)
    queries = dot(normed, w_query).astype(bf16)
    doc_keys = dot(normed, w_key).astype(bf16)
    doc_values = dot(normed, w_value).astype(bf16)
    ctx_keys = dot(ctx_normed, w_key).astype(bf16)
    ctx_values = dot(ctx_normed, w_value).astype(bf16)
    everyones = lax.all_gather(
        jnp.concatenate([queries, doc_keys, doc_values], axis=1), DP, axis=0, tiled=True
    )

    own_q, own_k, own_v = (a.reshape(docs, DOC_LEN, HD) for a in (queries, doc_keys, doc_values))
    ctx_probs, own_probs = probabilities(own_q, own_k, ctx_keys)
    mixture = ein("blc,ce->ble", ctx_probs.astype(bf16), ctx_values)
    mixture = mixture + ein("blm,bme->ble", own_probs.astype(bf16), own_v)
    mean_mixture = jnp.mean(wide(mixture.astype(bf16)), axis=1)
    branch = split_dot(mean_mixture, w_out, 3)
    branch = lax.psum(lax.psum(branch, "x"), "zh")
    pooled = jnp.mean(rows.reshape(docs, DOC_LEN, width), axis=1) + branch

    extra = jnp.concatenate([doc_inv.reshape(docs, DOC_LEN), wide(partners)[:, None]], axis=1)
    extra = jnp.pad(extra, ((0, 0), (0, HD - extra.shape[1])))
    message = jnp.concatenate([pooled, mean_mixture, extra], axis=1)
    message = spread(message, DP, n_dp).reshape(n_dp * docs, -1)
    pooled = message[:, :width]
    mean_mixture = message[:, width : width + HD]
    doc_inv = message[:, width + HD : width + HD + DOC_LEN]
    partners = message[:, width + HD + DOC_LEN].astype(jnp.int32)
    total = n_dp * docs

    length = jnp.sqrt(jnp.sum(pooled * pooled, axis=1) + 1e-06)
    unit = pooled / length[:, None]
    gram = jnp.dot(pooled, pooled.T, precision=EXACT)
    scores = gram / (length[:, None] * length[None, :]) / TEMPERATURE
    ids = jnp.arange(total, dtype=jnp.int32)
    exps = jnp.where(ids[:, None] != ids[None, :], jnp.exp(scores), 0.0)
    sums = jnp.sum(exps, axis=1)
    chosen = (partners[:, None] == ids[None, :]).astype(f32)
    loss = jnp.mean(jnp.log(sums) - jnp.sum(scores * chosen, axis=1))
    coeff = (exps / sums[:, None] - chosen) / total * LOSS_SCALE
    grad_unit = jnp.dot(coeff + coeff.T, unit, precision=EXACT) / TEMPERATURE
    radial = jnp.sum(unit * grad_unit, axis=1, keepdims=True)
    grad_pooled = (grad_unit - unit * radial) / length[:, None]
    grad_part = lax.dynamic_slice_in_dim(grad_pooled, dp_id * feat, feat, 1)
    grad_out = jnp.dot(mean_mixture.T, grad_part, precision=EXACT)
    grad_mixture = split_dot(grad_pooled / DOC_LEN, w_out.T, 3).astype(bf16)

    factor = HD**-0.5
    all_q, all_k, all_v = (
        everyones[:, i * HD : (i + 1) * HD].reshape(total, DOC_LEN, HD) for i in range(3)
    )
    ctx_probs, own_probs = probabilities(all_q, all_k, ctx_keys)
    ctx_dweights = ein("be,ce->bc", grad_mixture, ctx_values)[:, None, :]
    own_dweights = ein("be,bme->bm", grad_mixture, all_v)[:, None, :]
    inner = jnp.sum(ctx_probs * ctx_dweights, -1, keepdims=True)
    inner = inner + jnp.sum(own_probs * own_dweights, -1, keepdims=True)
    ctx_dscores = (ctx_probs * (ctx_dweights - inner) * factor).astype(bf16)
    own_dscores = (own_probs * (own_dweights - inner) * factor).astype(bf16)
    grad_queries = ein("blc,ce->ble", ctx_dscores, ctx_keys)
    grad_queries = (grad_queries + ein("blm,bme->ble", own_dscores, all_k)).astype(bf16)
    grad_keys = ein("blm,ble->bme", own_dscores, all_q).astype(bf16)
    own_weights = jnp.sum(wide(own_probs.astype(bf16)), axis=1)
    grad_values = (own_weights[:, :, None] * wide(grad_mixture)[:, None, :]).astype(bf16)
    ctx_weights = jnp.sum(wide(ctx_probs.astype(bf16)), axis=1)
    grad_ctx_keys = ein("blc,ble->ce", ctx_dscores, all_q)
    grad_ctx_values = jnp.dot(ctx_weights.T, wide(grad_mixture), precision=EXACT)

    half = width // 2
    key_half = lax.dynamic_slice_in_dim(w_key, co_id * half, half, 0)
    value_half = lax.dynamic_slice_in_dim(w_value, co_id * half, half, 0)
    part = split_dot(grad_ctx_keys, key_half.T, 2) + split_dot(grad_ctx_values, value_half.T, 2)
    part = part.astype(bf16).reshape(4, 4, -1, half).transpose(1, 0, 2, 3)
    part = jnp.sum(wide(lax.all_to_all(part, "x", 0, 0)), axis=0)
    part = jnp.sum(lax.all_to_all(part, "zh", 0, 0), axis=0)
    both = lax.all_gather(part, "co", axis=1, tiled=True)
    scaled = gain * both
    grad_context = own_ctx_inv * scaled - own_ctx * own_ctx_inv**3 * jnp.mean(
        own_ctx * scaled, axis=1, keepdims=True
    )

    gain_part = lax.dynamic_slice_in_dim(gain, dp_id * feat, feat, 0)
    columns = (wide(columns) * doc_inv.reshape(-1, 1) * gain_part).astype(bf16)
    ctx_columns = lax.dynamic_slice_in_dim(ctx_normed, dp_id * feat, feat, 1)
    grads = jnp.concatenate([grad_queries, grad_keys, grad_values], axis=2)
    grads = dot(columns.T, grads.reshape(-1, 3 * HD))
    from_ctx = split_dot(
        jnp.concatenate([grad_ctx_keys, grad_ctx_values], axis=1).T, ctx_columns, 2
    ).T
    grad_query = grads[:, :HD]
    grad_key = grads[:, HD : 2 * HD] + from_ctx[:, :HD]
    grad_value = grads[:, 2 * HD :] + from_ctx[:, HD:]
    return loss, grad_context, grad_query, grad_key, grad_value, grad_out


def solution(mesh):
    split = Mesh(mesh.devices.reshape(4, 4, 2, 4, 2), EVERY)
    in_specs = (
        P(DP, CTX),
        P(CTX, None),
        P(),
        P(None, CTX),
        P(None, CTX),
        P(None, CTX),
        P(CTX, None),
        P(DP),
    )
    out_specs = (P(), P(CTX, None), P(DP, CTX), P(DP, CTX), P(DP, CTX), P(CTX, DP))
    return jax.shard_map(
        shards, mesh=split, in_specs=in_specs, out_specs=out_specs, check_vma=False
    )
```

time: 900 us -> 338 us (0.38)
  waiting for transfers between devices: 691 us -> 198 us
  blocking collectives: 123 us -> 23.4 us
  starting transfers between devices: 0.54 us -> 30.7 us
  local copies, waits for them, and re-layouts: 10.6 us -> 21.6 us
  matrix products: 37.1 us -> 27.3 us
    reduce_scatter x4 -> x0, waiting for transfers between devices: 300 us -> none  [the longest x1 91.7 us: shards(): branch = lax.psum_scatter(branch, 'ctx', scatter_dimension=1, tiled=True)]
    all_gather x3, waiting for transfers between devices: 202 us -> 74.9 us  [the longest x1 35.4 us: shards(): lax.all_gather(lax.ppermute(doc_states, EVERY, swap), CTX, axis=0, tiled=...]
    unnamed x10 -> x5, waiting for transfers between devices: 111 us -> 0.08 us
    psum x3 -> x0, blocking collectives: 103 us -> none  [the longest x1 37.8 us: shards(): radial = lax.psum(jnp.sum(unit_mine * direction_loss_slope, axis=1), 'ctx')]
    ppermute x0 -> x2, waiting for transfers between devices: none -> 21.4 us  [the longest x1 18.7 us: shards(): lax.ppermute(own_ctx_normed, EVERY, swap)]
    all_to_all x0 -> x4, waiting for transfers between devices: none -> 20.5 us  [the longest x2 13.1 us: spread(): return lax.all_to_all(copies, axis, 0, 0)]
    all_to_all x0 -> x4, starting transfers between devices: none -> 19.9 us  [the longest x2 11.2 us: spread(): return lax.all_to_all(copies, axis, 0, 0)]
    convert_element_type x0 -> x2, local copies, waits for them, and re-layouts: none -> 11.2 us  [wide(): return a.astype(f32)]
  transfers between devices with their start and end apart: 9 -> 11, of which waited for: 9 -> 9; matrix products, arithmetic and copies ran while one was open for 4% -> 18% of each run, Pallas kernels for 0% -> 0%
where the time goes in v1:
time: 338 us; the launch traced here: 337 us
  waiting for transfers between devices  198 us (59%)
  starting transfers between devices  30.7 us (9%)
  matrix products  27.3 us (8%)
  blocking collectives  23.4 us (7%)
  local copies, waits for them, and re-layouts  21.6 us (6%)
  other arithmetic  19.8 us (6%)
  between operations  16.1 us (5%)
    psum x2, waiting for transfers between devices, shards(): branch = lax.psum(lax.psum(branch, 'x'), 'zh')  81.3 us
    all_gather x1, waiting for transfers between devices, shards(): lax.all_gather(lax.ppermute(doc_states, EVERY, swap), CTX, axis=0, tiled=...  35.4 us
    all_gather x1, waiting for transfers between devices, shards(): lax.all_gather(lax.ppermute(own_ctx_normed, EVERY, swap), DP, axis=0, til...  25.7 us
    ppermute x1, waiting for transfers between devices, shards(): lax.ppermute(own_ctx_normed, EVERY, swap)  18.7 us
    all_gather x1, blocking collectives, shards(): by_zh = lax.all_gather(doc_states, 'zh')  18.4 us
    all_gather x1, waiting for transfers between devices, shards(): lax.all_gather(jnp.concatenate([queries, doc_keys, doc_values], axis=1),...  13.8 us
    all_to_all x2, waiting for transfers between devices, spread(): return lax.all_to_all(copies, axis, 0, 0)  13.1 us
    dot_general x11, matrix products, dot(): return jnp.dot(a, b, preferred_element_type=f32)  12.4 us
  transfers between devices with their start and end apart: 11, of which 9 were waited for; matrix products, arithmetic and copies ran while one was open for 18% of the time, Pallas kernels for 0%

profile of v1, /device:TPU:1, one launch (start us, length us, event | category | flops | bytes accessed | tf_op | source)
XLA Modules:
  0.0 337.1 jit_solution(11129172677949689877)
XLA Ops:
  7.2 18.4 %all-gather = bf16[1024,256]{1,0:T(8,128)(2,1)S(1)} all-gather(bf16[256,256]{1,0:T(8,128)(2,1)} %param.8), channel_id=2, replica_groups=mesh['zh'=4,'x'=4,'zl'=2,'y'=4,'co'=2] {'zh'}, dimensions={0}, use_global_device_ids=true | all-gather | bytes 655360 | tf_op jit(solution)/shard_map/all_gather | solution.py:82
  25.8 1.5 broadcast_in_dim.9
  27.3 4.1 %all-to-all-start = ((bf16[4,4,256,256]{2,3,1,0:T(8,128)(2,1)}), bf16[4,4,256,256]{2,3,1,0:T(8,128)(2,1)S(1)}, u32[]{:S(2)}, u32[]{:S(2)}) async-start(bf16[4,4,256,256]{2,3,1,0:T(8,128)(2,1)} %broadcast_in_dim.9), calls=%async_computation | async-start | bytes 4194304 | tf_op jit(solution)/shard_map/all_to_all | solution.py:55
  31.6 0.5 multiply_multiply_fusion
  32.2 7.3 %collective-permute-start = (bf16[8,4096]{1,0:T(8,128)(2,1)S(1)}, bf16[8,4096]{1,0:T(8,128)(2,1)S(1)}, u32[]{:S(2)}, u32[]{:S(2)}) collective-permute-start(bf16[8,4096]{1,0:T(8,128)(2,1)S(1)} %fusion.37), channel_id=1, source_target_pairs={{0,0},{1,16},{2,32},{3,48},{4,64},{5,80},{6,96},{7,112},{8,128},{9... | collective-permute-start | bytes 196616 | tf_op jit(solution)/shard_map/ppermute | solution.py:79
  39.6 18.7 %collective-permute-done = bf16[8,4096]{1,0:T(8,128)(2,1)S(1)} collective-permute-done((bf16[8,4096]{1,0:T(8,128)(2,1)S(1)}, bf16[8,4096]{1,0:T(8,128)(2,1)S(1)}, u32[]{:S(2)}, u32[]{:S(2)}) %collective-permute-start) | collective-permute-done | bytes 65568 | tf_op jit(solution)/shard_map/ppermute | solution.py:79
  58.3 0.6 copy-done.18
  59.0 0.6 multiply_reduce_fusion
  59.6 2.5 fusion.9
  62.1 1.0 fusion.1
  63.3 0.8 convolution_convert_fusion.3
  64.1 0.8 convolution_convert_fusion.2
  64.8 0.8 fusion.122
  65.7 0.8 convolution_convert_fusion.1
  66.4 25.7 %all-gather.5.cloned.1.call-done = bf16[128,4096]{1,0:T(8,128)(2,1)} async-done(((bf16[8,4096]{1,0:T(8,128)(2,1)}), bf16[128,4096]{1,0:T(8,128)(2,1)}) %all-gather.5.cloned.1.call-update) | async-done | bytes 1048592 | tf_op jit(solution)/shard_map/all_gather | solution.py:79
  92.2 1.7 fusion.21
  94.2 0.4 convolution_convert_fusion.4
  95.4 0.7 slice_add_fusion.5
  96.1 43.6 %all-reduce.4.cloned.1.call-done = f32[4,4096]{1,0:T(4,128)} async-done(((f32[4,4096]{1,0:T(4,128)}), f32[4,4096]{1,0:T(4,128)}) %all-reduce.4.cloned.1.call-update) | async-done | bytes 65552 | tf_op jit(solution)/shard_map/psum | solution.py:101
  139.8 0.7 pad_maximum_fusion.1
  140.8 5.5 %copy.40 = f32[256,4,4,256]{3,2,1,0:T(4,128)} copy(f32[256,4,4,256]{0,3,2,1:T(8,128)} %get-tuple-element.19) | data formatting | bytes 8388608 | tf_op jit(solution)/shard_map/convert_element_type | solution.py:23
  146.2 5.8 %reshape.126 = f32[4,64,4096]{2,1,0:T(8,128)} reshape(f32[256,4,4,256]{3,2,1,0:T(4,128)} %copy.40) | data formatting | bytes 8388608 | tf_op jit(solution)/shard_map/convert_element_type | solution.py:23
  152.0 2.5 reduce_sum.180
  154.6 37.7 %all-reduce.6.cloned.1.call-done = f32[4,4096]{1,0:T(4,128)} async-done(((f32[4,4096]{1,0:T(4,128)}), f32[4,4096]{1,0:T(4,128)}) %all-reduce.6.cloned.1.call-update) | async-done | bytes 65552 | tf_op jit(solution)/shard_map/psum | solution.py:101
  192.3 0.9 multiply_add_fusion
  193.2 1.2 broadcast_in_dim.11
  194.4 7.1 %all-to-all-start.1 = ((f32[16,4,4352]{2,1,0:T(4,128)}), f32[16,4,4352]{2,1,0:T(4,128)}, u32[]{:S(2)}, u32[]{:S(2)}) async-start(f32[16,4,4352]{2,1,0:T(4,128)} %broadcast_in_dim.11), calls=%async_computation.1 | async-start | bytes 2228224 | tf_op jit(solution)/shard_map/all_to_all | solution.py:55
  201.6 3.3 collective-permute-start.1
  204.9 0.6 dynamic_slice.17
  205.5 2.7 collective-permute-done.1
  208.2 0.7 copy-done.16
  208.9 13.1 %all-to-all-done.1 = f32[16,4,4352]{2,1,0:T(4,128)} async-done(((f32[16,4,4352]{2,1,0:T(4,128)}), f32[16,4,4352]{2,1,0:T(4,128)}, u32[]{:S(2)}, u32[]{:S(2)}) %all-to-all-start.1) | async-done | bytes 1114144 | tf_op jit(solution)/shard_map/all_to_all | solution.py:55
  222.0 1.6 reshape.120
  223.7 1.0 fusion.26
  225.3 1.3 multiply_reduce_fusion.3
  227.0 1.0 fusion.56
  228.2 0.6 fusion.10
  229.0 0.6 subtract_reduce_fusion
  230.3 13.8 %all-gather.7.cloned.1.call-done = bf16[4096,384]{1,0:T(8,128)(2,1)} async-done(((bf16[256,384]{1,0:T(8,128)(2,1)}), bf16[4096,384]{1,0:T(8,128)(2,1)}) %all-gather.7.cloned.1.call-update) | async-done | bytes 3145744 | tf_op jit(solution)/shard_map/all_gather | solution.py:91
  244.1 2.1 fusion.120
  246.2 0.8 fusion.6
  247.0 0.7 fusion.8
  247.7 0.6 fusion.72
  248.4 1.4 convert_reduce_fusion
  249.8 1.4 multiply_reduce_fusion.2
  251.2 2.4 reduce-precision_convert_fusion.4
  253.6 0.4 fusion.30
  254.3 0.4 fusion.28
  255.0 0.8 copy.61
  255.9 5.2 %all-to-all-start.2 = ((bf16[4,4,8,2048]{3,2,1,0:T(8,128)(2,1)}), bf16[4,4,8,2048]{3,2,1,0:T(8,128)(2,1)S(1)}, u32[]{:S(2)}, u32[]{:S(2)}) async-start(bf16[4,4,8,2048]{3,2,1,0:T(8,128)(2,1)} %bitcast.78), calls=%async_computation.2 | async-start | bytes 1048576 | tf_op jit(solution)/shard_map/all_to_all | solution.py:156
  261.1 1.3 fusion.41
  262.4 0.7 multiply_convert_fusion.2
  263.1 2.6 fusion.45
  265.7 1.0 convolution_convert_fusion
  266.9 1.6 add_convert_fusion
  268.5 2.1 pad_maximum_fusion
  270.7 35.4 %all-gather.9.cloned.1.call-done = bf16[4096,256]{1,0:T(8,128)(2,1)} async-done(((bf16[256,256]{1,0:T(8,128)(2,1)}), bf16[4096,256]{1,0:T(8,128)(2,1)}) %all-gather.9.cloned.1.call-update) | async-done | bytes 2097168 | tf_op jit(solution)/shard_map/all_gather | solution.py:80
  306.1 5.1 %fusion.2 = f32[256,384]{1,0:T(8,128)S(1)} fusion(bf16[4096,384]{1,0:T(8,128)(2,1)} %bitcast.85, bf16[4096,256]{1,0:T(8,128)(2,1)} %all-gather.9.cloned.1.call-done, f32[256]{0:T(256)S(1)} %copy-done.22, f32[4096]{0:T(1024)S(1)} %mul.238), kind=kOutput, calls=%fused_computation.7 | convolution fusion | flops 809500672 | bytes 5653504 | tf_op jit(solution)/shard_map/dot_general | solution.py:36
  311.2 0.8 convert_reduce_fusion.2
  311.9 3.4 %all-to-all-start.3 = ((f32[4,8,2048]{2,1,0:T(8,128)}), f32[4,8,2048]{2,1,0:T(8,128)S(1)}, u32[]{:S(2)}, u32[]{:S(2)}) async-start(f32[4,8,2048]{2,1,0:T(8,128)} %convert_reduce_fusion.2), calls=%async_computation.3 | async-start | bytes 524288 | tf_op jit(solution)/shard_map/all_to_all | solution.py:157
  315.4 0.8 slice_add_fusion.3
  316.1 7.3 %all-to-all-done.3 = f32[4,8,2048]{2,1,0:T(8,128)S(1)} async-done(((f32[4,8,2048]{2,1,0:T(8,128)}), f32[4,8,2048]{2,1,0:T(8,128)S(1)}, u32[]{:S(2)}, u32[]{:S(2)}) %all-to-all-start.3) | async-done | bytes 262176 | tf_op jit(solution)/shard_map/all_to_all | solution.py:157
  323.5 5.0 %all_gather.22 = f32[8,4096]{1,0:T(8,128)S(1)} all-gather(f32[8,2048]{1,0:T(8,128)S(1)} %reduce_sum.197), channel_id=1, replica_groups=mesh['zh'=4,'x'=4,'zl'=2,'y'=4,'co'=2] {'co'}, dimensions={1}, use_global_device_ids=true | all-gather | bytes 196608 | tf_op jit(solution)/shard_map/all_gather | solution.py:158
  328.7 0.7 fusion.39
  (96 shorter events, 4.8 us)
Async XLA Ops:
  7.2 56.9 %copy-start = (bf16[4096,128]{1,0:T(8,128)(2,1)S(1)}, bf16[4096,128]{1,0:T(8,128)(2,1)}, u32[]{:S(2)}) copy-start(bf16[4096,128]{1,0:T(8,128)(2,1)} %param.12) | copy-start | bytes 3145732
  27.3 4.2 %copy-start.13 = (bf16[8,4096]{1,0:T(8,128)(2,1)S(1)}, bf16[8,4096]{1,0:T(8,128)(2,1)}, u32[]{:S(2)}) copy-start(bf16[8,4096]{1,0:T(8,128)(2,1)} %param.9) | copy-start | bytes 196612
  27.3 4.8 %copy-start.14 = (f32[4096]{0:T(1024)S(1)}, f32[4096]{0:T(1024)}, u32[]{:S(2)}) copy-start(f32[4096]{0:T(1024)} %param.10) | copy-start | bytes 49156
  27.3 31.6 %all-to-all-start = ((bf16[4,4,256,256]{2,3,1,0:T(8,128)(2,1)}), bf16[4,4,256,256]{2,3,1,0:T(8,128)(2,1)S(1)}, u32[]{:S(2)}, u32[]{:S(2)}) async-start(bf16[4,4,256,256]{2,3,1,0:T(8,128)(2,1)} %broadcast_in_dim.9), calls=%async_computation | async-start | bytes 4194304 | tf_op jit(solution)/shard_map/all_to_all | solution.py:55
  31.5 60.7 %all-gather.5.cloned.1.call-start = ((), (), s32[]{:S(2)}) async-start(), calls=%async_computation.4 | async-start | bytes 1114112 | tf_op jit(solution)/shard_map/all_gather | solution.py:79
  32.1 29.9 %copy-start.20 = (f32[8]{0:T(128)}, f32[8]{0:T(128)S(1)}, u32[]{:S(2)}) copy-start(f32[8]{0:T(128)S(1)} %get-tuple-element.37) | copy-start | bytes 100
  32.2 26.0 %collective-permute-start = (bf16[8,4096]{1,0:T(8,128)(2,1)S(1)}, bf16[8,4096]{1,0:T(8,128)(2,1)S(1)}, u32[]{:S(2)}, u32[]{:S(2)}) collective-permute-start(bf16[8,4096]{1,0:T(8,128)(2,1)S(1)} %fusion.37), channel_id=1, source_target_pairs={{0,0},{1,16},{2,32},{3,48},{4,64},{5,80},{6,96},{7,112},{8,128},{9... | collective-permute-start | bytes 196616 | tf_op jit(solution)/shard_map/ppermute | solution.py:79
  58.3 0.6 copy-start.18
  58.9 80.8 %all-reduce.4.cloned.1.call-start = ((), (), s32[]{:S(2)}) async-start(), calls=%async_computation.5 | async-start | bytes 131072 | tf_op jit(solution)/shard_map/psum | solution.py:101
  62.1 1.2 copy-start.10
  64.1 1.6 copy-start.6
  92.1 2.1 copy-start.7
  92.1 2.7 copy-start.17
  93.9 1.2 copy-start.11
  94.6 45.9 %copy-start.24 = (s32[4]{0:T(128)S(1)}, s32[4]{0:T(128)}, u32[]{:S(2)}) copy-start(s32[4]{0:T(128)} %param.15) | copy-start | bytes 52
  96.1 96.2 %all-reduce.6.cloned.1.call-start = ((), (), s32[]{:S(2)}) async-start(), calls=%async_computation.6 | async-start | bytes 131072 | tf_op jit(solution)/shard_map/psum | solution.py:101
  139.8 104.3 %all-gather.7.cloned.1.call-start = ((), (), s32[]{:S(2)}) async-start(), calls=%async_computation.7 | async-start | bytes 3342336 | tf_op jit(solution)/shard_map/all_gather | solution.py:91
  154.6 47.0 %copy-start.15 = (bf16[256,256]{1,0:T(8,128)(2,1)S(1)}, bf16[256,256]{1,0:T(8,128)(2,1)}, u32[]{:S(2)}) copy-start(bf16[256,256]{1,0:T(8,128)(2,1)} %param.8) | copy-start | bytes 393220
  194.4 27.7 %all-to-all-start.1 = ((f32[16,4,4352]{2,1,0:T(4,128)}), f32[16,4,4352]{2,1,0:T(4,128)}, u32[]{:S(2)}, u32[]{:S(2)}) async-start(f32[16,4,4352]{2,1,0:T(4,128)} %broadcast_in_dim.11), calls=%async_computation.1 | async-start | bytes 2228224 | tf_op jit(solution)/shard_map/all_to_all | solution.py:55
  201.5 104.6 %all-gather.9.cloned.1.call-start = ((), (), s32[]{:S(2)}) async-start(), calls=%async_computation.8 | async-start | bytes 2228224 | tf_op jit(solution)/shard_map/all_gather | solution.py:80
  201.6 6.7 %collective-permute-start.1 = (bf16[256,256]{1,0:T(8,128)(2,1)S(1)}, bf16[256,256]{1,0:T(8,128)(2,1)S(1)}, u32[]{:S(2)}, u32[]{:S(2)}) collective-permute-start(bf16[256,256]{1,0:T(8,128)(2,1)S(1)} %copy-done.15), channel_id=1, source_target_pairs={{0,0},{1,16},{2,32},{3,48},{4,64},{5,80},{6,96},{7,112},{8,128},{9... | collective-permute-start | bytes 393224 | tf_op jit(solution)/shard_map/ppermute | solution.py:80
  208.2 0.7 copy-start.16
  223.7 4.5 %copy-start.1 = (f32[64,4352]{1,0:T(8,128)}, f32[64,4352]{1,0:T(8,128)S(1)}, u32[]{:S(2)}) copy-start(f32[64,4352]{1,0:T(8,128)S(1)} %reshape.120) | copy-start | bytes 3342340
  226.9 1.3 copy-start.12
  228.2 0.8 slice-start
  246.2 1.5 copy-start.8
  247.0 4.2 %copy-start.4 = (f32[64,64,128]{2,1,0:T(8,128)}, f32[64,64,128]{2,1,0:T(8,128)S(1)}, u32[]{:S(2)}) copy-start(f32[64,64,128]{2,1,0:T(8,128)S(1)} %get-tuple-element.45) | copy-start | bytes 6291460
  247.7 3.5 %copy-start.2 = (f32[64,64,64]{1,2,0:T(8,128)}, f32[64,64,64]{1,2,0:T(8,128)S(1)}, u32[]{:S(2)}) copy-start(f32[64,64,64]{1,2,0:T(8,128)S(1)} %get-tuple-element.47) | copy-start | bytes 3145732
  255.0 6.1 %copy-start.19 = (f32[128,128]{1,0:T(8,128)S(1)}, f32[128,128]{1,0:T(8,128)}, u32[]{:S(2)}) copy-start(f32[128,128]{1,0:T(8,128)} %get-tuple-element.49) | copy-start | bytes 196612
  255.9 55.3 %all-to-all-start.2 = ((bf16[4,4,8,2048]{3,2,1,0:T(8,128)(2,1)}), bf16[4,4,8,2048]{3,2,1,0:T(8,128)(2,1)S(1)}, u32[]{:S(2)}, u32[]{:S(2)}) async-start(bf16[4,4,8,2048]{3,2,1,0:T(8,128)(2,1)} %bitcast.78), calls=%async_computation.2 | async-start | bytes 1048576 | tf_op jit(solution)/shard_map/all_to_all | solution.py:156
  261.1 2.0 copy-start.5
  263.1 2.6 copy-start.3
  265.7 1.2 copy-start.9
  268.5 37.5 %copy-start.22 = (f32[256]{0:T(256)S(1)}, f32[256]{0:T(256)}, u32[]{:S(2)}) copy-start(f32[256]{0:T(256)} %dynamic_slice.17) | copy-start | bytes 3076
  311.1 17.5 %copy-start.21 = (f32[8]{0:T(128)S(1)}, f32[8]{0:T(128)}, u32[]{:S(2)}) copy-start(f32[8]{0:T(128)} %copy-done.20) | copy-start | bytes 100
  311.1 17.5 %copy-start.23 = (f32[8]{0:T(128)S(1)}, f32[8]{0:T(128)}, u32[]{:S(2)}) copy-start(f32[8]{0:T(128)} %get-tuple-element.36) | copy-start | bytes 100
  311.9 11.5 %all-to-all-start.3 = ((f32[4,8,2048]{2,1,0:T(8,128)}), f32[4,8,2048]{2,1,0:T(8,128)S(1)}, u32[]{:S(2)}, u32[]{:S(2)}) async-start(f32[4,8,2048]{2,1,0:T(8,128)} %convert_reduce_fusion.2), calls=%async_computation.3 | async-start | bytes 524288 | tf_op jit(solution)/shard_map/all_to_all | solution.py:157
Sparse Core Ops, SparseCore 0:
  59.0 33.0 all-gather.4
  96.2 43.5 all-reduce.3
  142.5 49.7 all-reduce.5
  194.0 50.0 all-gather.6
  247.0 59.0 all-gather.8

commit v2 on v1

--- a/solution.py
+++ b/solution.py
@@ -76,8 +76,15 @@
     own_ctx = wide(context)
     own_ctx_inv = inverse_rms(own_ctx)
     own_ctx_normed = (own_ctx * own_ctx_inv * gain).astype(bf16)
-    ctx_normed = lax.all_gather(lax.ppermute(own_ctx_normed, EVERY, swap), DP, axis=0, tiled=True)
-    columns = lax.all_gather(lax.ppermute(doc_states, EVERY, swap), CTX, axis=0, tiled=True)
+    named_rows = lax.ppermute(own_ctx_normed, EVERY, swap)
+    few = jnp.concatenate([dot(named_rows, w_key), dot(named_rows, w_value)], axis=1).astype(bf16)
+    few = spread(few, DP, n_dp).reshape(-1, 2 * HD)
+    ctx_keys, ctx_values = few[:, :HD], few[:, HD:]
+    ctx_part = lax.dynamic_slice_in_dim(own_ctx_normed, dp_id * feat, feat, 1)
+    columns = lax.ppermute(doc_states, EVERY, swap)
+    columns = lax.all_gather(jnp.concatenate([columns, ctx_part], axis=0), CTX)
+    ctx_columns = columns[:, tok:].reshape(-1, feat)
+    columns = columns[:, :tok].reshape(-1, feat)
 
     by_zh = lax.all_gather(doc_states, "zh")
     rows = wide(spread(by_zh, "x", 4).transpose(2, 1, 0, 3).reshape(tok, width))
@@ -86,8 +93,6 @@
     queries = dot(normed, w_query).astype(bf16)
     doc_keys = dot(normed, w_key).astype(bf16)
     doc_values = dot(normed, w_value).astype(bf16)
-    ctx_keys = dot(ctx_normed, w_key).astype(bf16)
-    ctx_values = dot(ctx_normed, w_value).astype(bf16)
     everyones = lax.all_gather(
         jnp.concatenate([queries, doc_keys, doc_values], axis=1), DP, axis=0, tiled=True
     )
@@ -98,7 +103,8 @@
     mixture = mixture + ein("blm,bme->ble", own_probs.astype(bf16), own_v)
     mean_mixture = jnp.mean(wide(mixture.astype(bf16)), axis=1)
     branch = split_dot(mean_mixture, w_out, 3)
-    branch = lax.psum(lax.psum(branch, "x"), "zh")
+    branch = jnp.sum(spread(branch, "x", 4), axis=0)
+    branch = jnp.sum(spread(branch, "zh", 4), axis=0)
     pooled = jnp.mean(rows.reshape(docs, DOC_LEN, width), axis=1) + branch
 
     extra = jnp.concatenate([doc_inv.reshape(docs, DOC_LEN), wide(partners)[:, None]], axis=1)
@@ -163,7 +169,6 @@
 
     gain_part = lax.dynamic_slice_in_dim(gain, dp_id * feat, feat, 0)
     columns = (wide(columns) * doc_inv.reshape(-1, 1) * gain_part).astype(bf16)
-    ctx_columns = lax.dynamic_slice_in_dim(ctx_normed, dp_id * feat, feat, 1)
     grads = jnp.concatenate([grad_queries, grad_keys, grad_values], axis=2)
     grads = dot(columns.T, grads.reshape(-1, 3 * HD))
     from_ctx = split_dot(

time: 338 us -> 230 us (0.68)
  waiting for transfers between devices: 198 us -> 65.6 us
  starting transfers between devices: 30.7 us -> 46.2 us
  blocking collectives: 23.4 us -> 35.6 us
  matrix products: 27.3 us -> 22 us
    psum x2 -> x0, waiting for transfers between devices: 81.3 us -> none  [shards(): branch = lax.psum(lax.psum(branch, 'x'), 'zh')]
    all_gather x2 -> x1, waiting for transfers between devices: 61.1 us -> 0.01 us  [shards(): columns = lax.all_gather(jnp.concatenate([columns, ctx_part], axis=0), CTX)]
    all_to_all x2 -> x4, starting transfers between devices: 11.2 us -> 26.9 us  [spread(): return lax.all_to_all(copies, axis, 0, 0)]
    all_to_all x0 -> x1, blocking collectives: none -> 9.25 us  [spread(): return lax.all_to_all(copies, axis, 0, 0)]
    dot_general x11, matrix products: 12.4 us -> 8.08 us  [dot(): return jnp.dot(a, b, preferred_element_type=f32)]
    all_to_all x1, waiting for transfers between devices: 0.01 us -> 4.32 us  [shards(): part = jnp.sum(wide(lax.all_to_all(part, 'x', 0, 0)), axis=0)]
    all_to_all x2 -> x4, waiting for transfers between devices: 13.1 us -> 17.4 us  [spread(): return lax.all_to_all(copies, axis, 0, 0)]
  transfers between devices with their start and end apart: 11 -> 10, of which waited for: 9 -> 5; matrix products, arithmetic and copies ran while one was open for 18% -> 19% of each run, Pallas kernels for 0% -> 0%
where the time goes in v2:
time: 230 us; the launch traced here: 229 us
  waiting for transfers between devices  65.6 us (29%)
  starting transfers between devices  46.2 us (20%)
  blocking collectives  35.6 us (15%)
  local copies, waits for them, and re-layouts  23.4 us (10%)
  matrix products  22 us (10%)
  other arithmetic  19.9 us (9%)
  between operations  16.3 us (7%)
    all_to_all x4, starting transfers between devices, spread(): return lax.all_to_all(copies, axis, 0, 0)  26.9 us
    ppermute x1, waiting for transfers between devices, shards(): named_rows = lax.ppermute(own_ctx_normed, EVERY, swap)  22.3 us
    all_gather x1, blocking collectives, shards(): by_zh = lax.all_gather(doc_states, 'zh')  21.3 us
    all_to_all x4, waiting for transfers between devices, spread(): return lax.all_to_all(copies, axis, 0, 0)  17.4 us
    all_gather x1, waiting for transfers between devices, shards(): lax.all_gather(jnp.concatenate([queries, doc_keys, doc_values], axis=1),...  14.2 us
    convert_element_type x2, local copies, waits for them, and re-layouts, wide(): return a.astype(f32)  11.4 us
    dot_general x12, matrix products, ein(): return jnp.einsum(form, a, b, preferred_element_type=f32)  10.4 us
    all_to_all x1, blocking collectives, spread(): return lax.all_to_all(copies, axis, 0, 0)  9.25 us
  transfers between devices with their start and end apart: 10, of which 5 were waited for; matrix products, arithmetic and copies ran while one was open for 19% of the time, Pallas kernels for 0%

profile of v2, /device:TPU:1, one launch (start us, length us, event | category | flops | bytes accessed | tf_op | source)
XLA Modules:
  0.0 229.1 jit_solution(4021336212740510370)
XLA Ops:
  7.2 4.6 %collective-permute-start.1 = (bf16[256,256]{1,0:T(8,128)(2,1)}, bf16[256,256]{1,0:T(8,128)(2,1)S(1)}, u32[]{:S(2)}, u32[]{:S(2)}) collective-permute-start(bf16[256,256]{1,0:T(8,128)(2,1)} %param.8), channel_id=1, source_target_pairs={{0,0},{1,16},{2,32},{3,48},{4,64},{5,80},{6,96},{7,112},{8,128},{9... | collective-permute-start | bytes 393224 | tf_op jit(solution)/shard_map/ppermute | solution.py:84
  11.8 21.3 %all-gather = bf16[1024,256]{1,0:T(8,128)(2,1)S(1)} all-gather(bf16[256,256]{1,0:T(8,128)(2,1)} %param.8), channel_id=2, replica_groups=mesh['zh'=4,'x'=4,'zl'=2,'y'=4,'co'=2] {'zh'}, dimensions={0}, use_global_device_ids=true | all-gather | bytes 655360 | tf_op jit(solution)/shard_map/all_gather | solution.py:89
  33.3 1.6 broadcast_in_dim.15
  34.9 3.7 %all-to-all-start = ((bf16[4,4,256,256]{2,3,1,0:T(8,128)(2,1)}), bf16[4,4,256,256]{2,3,1,0:T(8,128)(2,1)S(1)}, u32[]{:S(2)}, u32[]{:S(2)}) async-start(bf16[4,4,256,256]{2,3,1,0:T(8,128)(2,1)} %broadcast_in_dim.15), calls=%async_computation | async-start | bytes 4194304 | tf_op jit(solution)/shard_map/all_to_all | solution.py:55
  38.9 4.1 %collective-permute-start = (bf16[8,4096]{1,0:T(8,128)(2,1)S(1)}, bf16[8,4096]{1,0:T(8,128)(2,1)S(1)}, u32[]{:S(2)}, u32[]{:S(2)}) collective-permute-start(bf16[8,4096]{1,0:T(8,128)(2,1)S(1)} %fusion.33), channel_id=1, source_target_pairs={{0,0},{1,16},{2,32},{3,48},{4,64},{5,80},{6,96},{7,112},{8,128},{9... | collective-permute-start | bytes 196616 | tf_op jit(solution)/shard_map/ppermute | solution.py:79
  43.1 22.3 %collective-permute-done = bf16[8,4096]{1,0:T(8,128)(2,1)S(1)} collective-permute-done((bf16[8,4096]{1,0:T(8,128)(2,1)S(1)}, bf16[8,4096]{1,0:T(8,128)(2,1)S(1)}, u32[]{:S(2)}, u32[]{:S(2)}) %collective-permute-start) | collective-permute-done | bytes 65568 | tf_op jit(solution)/shard_map/ppermute | solution.py:79
  65.4 1.5 convolution_convert_fusion.4
  67.1 0.7 pad_maximum_fusion.2
  67.8 0.6 broadcast_in_dim.16
  68.5 7.8 %all-to-all-start.1 = ((bf16[16,8,256]{2,1,0:T(8,128)(2,1)}), bf16[16,8,256]{2,1,0:T(8,128)(2,1)S(1)}, u32[]{:S(2)}, u32[]{:S(2)}) async-start(bf16[16,8,256]{2,1,0:T(8,128)(2,1)} %broadcast_in_dim.16), calls=%async_computation.1 | async-start | bytes 131072 | tf_op jit(solution)/shard_map/all_to_all | solution.py:55
  76.3 0.6 multiply_reduce_fusion
  76.9 2.5 %fusion.6 = (f32[256,4,4,256]{0,3,2,1:T(8,128)}, f32[4,4,256,256]{2,3,0,1:T(8,128)S(1)}) fusion(bf16[4,4,256,256]{2,3,1,0:T(8,128)(2,1)S(1)} %all-to-all-done), kind=kLoop, calls=%fused_computation.22 | loop fusion | flops 1048576 | bytes 10485760 | tf_op jit(solution)/shard_map/convert_element_type | solution.py:23
  79.4 1.0 fusion.1
  80.4 0.8 convolution_convert_fusion.2
  81.1 0.5 copy-done.1
  81.6 0.8 convolution_convert_fusion.1
  82.4 0.5 copy-done.3
  82.8 0.8 convolution_convert_fusion.3
  84.9 9.3 %all_to_all.35 = f32[4,4,4096]{2,1,0:T(4,128)S(1)} all-to-all(f32[4,4,4096]{2,1,0:T(4,128)S(1)} %broadcast_in_dim.17), channel_id=1, replica_groups=mesh['zh'=4,'x'=4,'zl'=2,'y'=4,'co'=2] {'x'}, dimensions={0} | all-to-all | bytes 524288 | tf_op jit(solution)/shard_map/all_to_all | solution.py:55
  94.2 0.7 broadcast_in_dim.18
  95.0 7.4 %all-to-all-start.3 = ((f32[4,4,4096]{2,1,0:T(4,128)}), f32[4,4,4096]{2,1,0:T(4,128)S(1)}, u32[]{:S(2)}, u32[]{:S(2)}) async-start(f32[4,4,4096]{2,1,0:T(4,128)} %broadcast_in_dim.18), calls=%async_computation.3 | async-start | bytes 524288 | tf_op jit(solution)/shard_map/all_to_all | solution.py:55
  102.5 5.6 %copy.40 = f32[256,4,4,256]{3,2,1,0:T(4,128)} copy(f32[256,4,4,256]{0,3,2,1:T(8,128)} %get-tuple-element.19) | data formatting | bytes 8388608 | tf_op jit(solution)/shard_map/convert_element_type | solution.py:23
  108.1 5.8 %reshape.163 = f32[4,64,4096]{2,1,0:T(8,128)} reshape(f32[256,4,4,256]{3,2,1,0:T(4,128)} %copy.40) | data formatting | bytes 8388608 | tf_op jit(solution)/shard_map/convert_element_type | solution.py:23
  113.9 2.6 %reduce_sum.198 = f32[4,4096]{1,0:T(4,128)S(1)} reduce(f32[4,64,4096]{2,1,0:T(8,128)} %reshape.163, f32[]{:T(128)} %constant.18.clone.1), dimensions={1}, to_apply=%region_0.0 | reduce | flops 1032192 | bytes 4259844 | tf_op jit(solution)/shard_map/reduce_sum | solution.py:108
  116.7 1.1 broadcast_in_dim.20
  117.8 8.0 %all-to-all-start.4 = ((f32[16,4,4352]{2,1,0:T(4,128)}), f32[16,4,4352]{2,1,0:T(4,128)}, u32[]{:S(2)}, u32[]{:S(2)}) async-start(f32[16,4,4352]{2,1,0:T(4,128)} %broadcast_in_dim.20), calls=%async_computation.4 | async-start | bytes 2228224 | tf_op jit(solution)/shard_map/all_to_all | solution.py:55
  126.0 0.7 pad_maximum_fusion.1
  126.8 17.4 %all-to-all-done.4 = f32[16,4,4352]{2,1,0:T(4,128)} async-done(((f32[16,4,4352]{2,1,0:T(4,128)}), f32[16,4,4352]{2,1,0:T(4,128)}, u32[]{:S(2)}, u32[]{:S(2)}) %all-to-all-start.4) | async-done | bytes 1114144 | tf_op jit(solution)/shard_map/all_to_all | solution.py:55
  144.2 1.6 reshape.156
  145.8 1.0 fusion.22
  147.6 0.6 subtract_reduce_fusion
  148.8 1.3 multiply_reduce_fusion.3
  150.7 0.7 copy-done.5
  151.4 0.6 fusion.7
  152.1 1.0 fusion.52
  153.1 3.0 %multiply_convert_fusion = bf16[16,256,256]{2,1,0:T(8,128)(2,1)} fusion(bf16[16,264,256]{2,1,0:T(8,128)(2,1)} %bitcast.96, f32[256]{0:T(256)S(1)} %dynamic_slice.18, f32[16,256]{1,0:T(8,128)S(1)} %mul.243), kind=kLoop, calls=%fused_computation.4 | loop fusion | flops 4194304 | bytes 4211712 | tf_op jit(solution)/shard_map/convert_element_type | solution.py:171
  156.0 14.2 %all-gather.5.cloned.1.call-done = bf16[4096,384]{1,0:T(8,128)(2,1)} async-done(((bf16[256,384]{1,0:T(8,128)(2,1)}), bf16[4096,384]{1,0:T(8,128)(2,1)}) %all-gather.5.cloned.1.call-update) | async-done | bytes 3145744 | tf_op jit(solution)/shard_map/all_gather | solution.py:96
  170.3 2.1 fusion.118
  172.3 0.8 fusion.3
  173.2 0.7 fusion.5
  173.8 0.6 fusion.67
  174.5 1.4 convert_reduce_fusion
  175.9 1.4 multiply_reduce_fusion.2
  177.3 1.3 fusion.41
  178.6 1.8 convolution_convert_fusion
  180.3 1.7 reduce-precision_convert_fusion.4
  182.1 2.4 %add_convert_fusion = bf16[64,64,128]{2,1,0:T(8,128)(2,1)} fusion(f32[64,64,128]{2,1,0:T(8,128)S(1)} %fusion.41, bf16[64,64,128]{2,1,0:T(8,128)(2,1)S(1)} %bitcast.94, f32[64,64]{1,0:T(8,128)S(1)} %add.136, f32[64,64]{1,0:T(8,128)S(1)} %bitcast.114, f32[64,64,64]{1,2,0:T(8,128)S(1)} %get-tuple-element.47, f32[64,64]{1,0:T(8,128)S(1)} %add.132), kind=kOutput, calls=%fused_computation.10 | convolution fusion | flops 69730304 | bytes 5292032 | tf_op jit(solution)/shard_map/blm,bme->ble/dot_general | solution.py:46
  184.8 0.4 fusion.26
  185.2 0.4 fusion.24
  185.7 0.3 fusion.21
  186.0 0.8 copy.61
  186.8 4.0 %all-to-all-start.5 = ((bf16[4,4,8,2048]{3,2,1,0:T(8,128)(2,1)}), bf16[4,4,8,2048]{3,2,1,0:T(8,128)(2,1)S(1)}, u32[]{:S(2)}, u32[]{:S(2)}) async-start(bf16[4,4,8,2048]{3,2,1,0:T(8,128)(2,1)} %bitcast.88), calls=%async_computation.5 | async-start | bytes 1048576 | tf_op jit(solution)/shard_map/all_to_all | solution.py:162
  190.9 0.7 multiply_convert_fusion.1
  191.6 1.1 fusion.37
  192.7 0.5 pad_maximum_fusion
  193.2 1.1 copy-done.2
  194.3 1.3 fusion.121
  195.6 4.3 %all-to-all-done.5 = bf16[4,4,8,2048]{3,2,1,0:T(8,128)(2,1)S(1)} async-done(((bf16[4,4,8,2048]{3,2,1,0:T(8,128)(2,1)}), bf16[4,4,8,2048]{3,2,1,0:T(8,128)(2,1)S(1)}, u32[]{:S(2)}, u32[]{:S(2)}) %all-to-all-start.5) | async-done | bytes 524320 | tf_op jit(solution)/shard_map/all_to_all | solution.py:162
  199.9 0.8 convert_reduce_fusion.2
  200.7 6.3 %all-to-all-start.6 = ((f32[4,8,2048]{2,1,0:T(8,128)}), f32[4,8,2048]{2,1,0:T(8,128)S(1)}, u32[]{:S(2)}, u32[]{:S(2)}) async-start(f32[4,8,2048]{2,1,0:T(8,128)} %convert_reduce_fusion.2), calls=%async_computation.6 | async-start | bytes 524288 | tf_op jit(solution)/shard_map/all_to_all | solution.py:163
  207.0 0.8 slice_add_fusion.3
  207.7 7.4 %all-to-all-done.6 = f32[4,8,2048]{2,1,0:T(8,128)S(1)} async-done(((f32[4,8,2048]{2,1,0:T(8,128)}), f32[4,8,2048]{2,1,0:T(8,128)S(1)}, u32[]{:S(2)}, u32[]{:S(2)}) %all-to-all-start.6) | async-done | bytes 262176 | tf_op jit(solution)/shard_map/all_to_all | solution.py:163
  215.1 5.1 %all_gather.21 = f32[8,4096]{1,0:T(8,128)S(1)} all-gather(f32[8,2048]{1,0:T(8,128)S(1)} %reduce_sum.217), channel_id=1, replica_groups=mesh['zh'=4,'x'=4,'zl'=2,'y'=4,'co'=2] {'co'}, dimensions={1}, use_global_device_ids=true | all-gather | bytes 196608 | tf_op jit(solution)/shard_map/all_gather | solution.py:164
  220.4 0.8 fusion.35
  (72 shorter events, 4.7 us)
Async XLA Ops:
  7.2 59.7 %copy-start = (bf16[4096,128]{1,0:T(8,128)(2,1)S(1)}, bf16[4096,128]{1,0:T(8,128)(2,1)}, u32[]{:S(2)}) copy-start(bf16[4096,128]{1,0:T(8,128)(2,1)} %param.12) | copy-start | bytes 3145732
  7.2 59.9 %collective-permute-start.1 = (bf16[256,256]{1,0:T(8,128)(2,1)}, bf16[256,256]{1,0:T(8,128)(2,1)S(1)}, u32[]{:S(2)}, u32[]{:S(2)}) collective-permute-start(bf16[256,256]{1,0:T(8,128)(2,1)} %param.8), channel_id=1, source_target_pairs={{0,0},{1,16},{2,32},{3,48},{4,64},{5,80},{6,96},{7,112},{8,128},{9... | collective-permute-start | bytes 393224 | tf_op jit(solution)/shard_map/ppermute | solution.py:84
  34.9 3.8 %copy-start.6 = (bf16[8,4096]{1,0:T(8,128)(2,1)S(1)}, bf16[8,4096]{1,0:T(8,128)(2,1)}, u32[]{:S(2)}) copy-start(bf16[8,4096]{1,0:T(8,128)(2,1)} %param.9) | copy-start | bytes 196612
  34.9 4.0 %copy-start.9 = (f32[4096]{0:T(1024)S(1)}, f32[4096]{0:T(1024)}, u32[]{:S(2)}) copy-start(f32[4096]{0:T(1024)} %param.10) | copy-start | bytes 49156
  34.9 32.9 %all-to-all-start = ((bf16[4,4,256,256]{2,3,1,0:T(8,128)(2,1)}), bf16[4,4,256,256]{2,3,1,0:T(8,128)(2,1)S(1)}, u32[]{:S(2)}, u32[]{:S(2)}) async-start(bf16[4,4,256,256]{2,3,1,0:T(8,128)(2,1)} %broadcast_in_dim.15), calls=%async_computation | async-start | bytes 4194304 | tf_op jit(solution)/shard_map/all_to_all | solution.py:55
  38.6 114.4 %all-gather.7.cloned.1.call-start = ((), (), s32[]{:S(2)}) async-start(), calls=%async_computation.8 | async-start | bytes 2297856 | tf_op jit(solution)/shard_map/all_gather | solution.py:85
  38.9 26.4 %collective-permute-start = (bf16[8,4096]{1,0:T(8,128)(2,1)S(1)}, bf16[8,4096]{1,0:T(8,128)(2,1)S(1)}, u32[]{:S(2)}, u32[]{:S(2)}) collective-permute-start(bf16[8,4096]{1,0:T(8,128)(2,1)S(1)} %fusion.33), channel_id=1, source_target_pairs={{0,0},{1,16},{2,32},{3,48},{4,64},{5,80},{6,96},{7,112},{8,128},{9... | collective-permute-start | bytes 196616 | tf_op jit(solution)/shard_map/ppermute | solution.py:79
  68.5 15.2 %all-to-all-start.1 = ((bf16[16,8,256]{2,1,0:T(8,128)(2,1)}), bf16[16,8,256]{2,1,0:T(8,128)(2,1)S(1)}, u32[]{:S(2)}, u32[]{:S(2)}) async-start(bf16[16,8,256]{2,1,0:T(8,128)(2,1)} %broadcast_in_dim.16), calls=%async_computation.1 | async-start | bytes 131072 | tf_op jit(solution)/shard_map/all_to_all | solution.py:55
  80.4 1.2 copy-start.1
  81.6 1.2 copy-start.3
  82.8 1.8 copy-start.4
  84.3 18.0 %copy-start.10 = (s32[4]{0:T(128)S(1)}, s32[4]{0:T(128)}, u32[]{:S(2)}) copy-start(s32[4]{0:T(128)} %param.15) | copy-start | bytes 52
  95.0 21.6 %all-to-all-start.3 = ((f32[4,4,4096]{2,1,0:T(4,128)}), f32[4,4,4096]{2,1,0:T(4,128)S(1)}, u32[]{:S(2)}, u32[]{:S(2)}) async-start(f32[4,4,4096]{2,1,0:T(4,128)} %broadcast_in_dim.18), calls=%async_computation.3 | async-start | bytes 524288 | tf_op jit(solution)/shard_map/all_to_all | solution.py:55
  117.8 26.4 %all-to-all-start.4 = ((f32[16,4,4352]{2,1,0:T(4,128)}), f32[16,4,4352]{2,1,0:T(4,128)}, u32[]{:S(2)}, u32[]{:S(2)}) async-start(f32[16,4,4352]{2,1,0:T(4,128)} %broadcast_in_dim.20), calls=%async_computation.4 | async-start | bytes 2228224 | tf_op jit(solution)/shard_map/all_to_all | solution.py:55
  125.8 44.5 %all-gather.5.cloned.1.call-start = ((), (), s32[]{:S(2)}) async-start(), calls=%async_computation.7 | async-start | bytes 3342336 | tf_op jit(solution)/shard_map/all_gather | solution.py:96
  150.1 1.2 copy-start.5
  186.0 6.7 %copy-start.7 = (bf16[64,64,128]{2,1,0:T(8,128)(2,1)S(1)}, bf16[64,64,128]{2,1,0:T(8,128)(2,1)}, u32[]{:S(2)}) copy-start(bf16[64,64,128]{2,1,0:T(8,128)(2,1)} %convolution_convert_fusion) | copy-start | bytes 3145732
  186.8 13.1 %all-to-all-start.5 = ((bf16[4,4,8,2048]{3,2,1,0:T(8,128)(2,1)}), bf16[4,4,8,2048]{3,2,1,0:T(8,128)(2,1)S(1)}, u32[]{:S(2)}, u32[]{:S(2)}) async-start(bf16[4,4,8,2048]{3,2,1,0:T(8,128)(2,1)} %bitcast.88), calls=%async_computation.5 | async-start | bytes 1048576 | tf_op jit(solution)/shard_map/all_to_all | solution.py:162
  190.9 1.8 copy-start.8
  192.7 1.6 copy-start.2
  200.7 14.4 %all-to-all-start.6 = ((f32[4,8,2048]{2,1,0:T(8,128)}), f32[4,8,2048]{2,1,0:T(8,128)S(1)}, u32[]{:S(2)}, u32[]{:S(2)}) async-start(f32[4,8,2048]{2,1,0:T(8,128)} %convert_reduce_fusion.2), calls=%async_computation.6 | async-start | bytes 524288 | tf_op jit(solution)/shard_map/all_to_all | solution.py:163
Sparse Core Ops, SparseCore 0:
  67.9 61.7 all-gather.6
  131.6 38.6 all-gather.4

commit v3 on v2

v3 whole, which is shorter than its diff:
```python
import jax
import jax.numpy as jnp
from jax import lax
from jax.sharding import Mesh, PartitionSpec as P

HD = 128
DOC_LEN = 64

EPS = 1e-05
TEMPERATURE = 0.05
LOSS_SCALE = 65536.0
EXACT = lax.Precision.HIGHEST

CTX = ("zh", "x")
DP = ("zl", "y", "co")
EVERY = CTX + DP

f32 = jnp.float32
bf16 = jnp.bfloat16


def wide(a):
    return a.astype(f32)


def pieces(a, count):
    out = []
    for _ in range(count):
        head = lax.reduce_precision(a, 8, 7)
        out.append(head.astype(bf16))
        a = a - head
    return out


def dot(a, b):
    return jnp.dot(a, b, preferred_element_type=f32)


def split_dot(a, b, count):
    rows = a.shape[0]
    got = dot(jnp.concatenate(pieces(a, count), axis=0), b)
    return sum(got[i * rows : (i + 1) * rows] for i in reversed(range(count)))


def ein(form, a, b):
    return jnp.einsum(form, a, b, preferred_element_type=f32)


def inverse_rms(a):
    return lax.rsqrt(jnp.mean(a * a, axis=-1, keepdims=True) + EPS)


def spread(block, axis, size):
    copies = jnp.broadcast_to(block[None], (size,) + block.shape)
    return lax.all_to_all(copies, axis, 0, 0)


def other_of_two(a, axis):
    return lax.ppermute(a, axis, [(0, 1), (1, 0)])


def pair(a, axis):
    b = other_of_two(a, axis)
    return jnp.where(lax.axis_index(axis) == 0, jnp.stack([a, b]), jnp.stack([b, a]))


def ring(a, axis):
    one, two, three = (
        lax.ppermute(a, axis, [(i, (i + k) % 4) for i in range(4)]) for k in (1, 2, 3)
    )
    cycle = jnp.stack([three, two, one, a, three, two, one])
    return lax.dynamic_slice_in_dim(cycle, 3 - lax.axis_index(axis), 4, 0)


def probabilities(queries, doc_keys, ctx_keys):
    factor = HD**-0.5
    ctx_exps = jnp.exp(ein("ble,ce->blc", queries, ctx_keys) * factor)
    own_exps = jnp.exp(ein("ble,bme->blm", queries, doc_keys) * factor)
    total = jnp.sum(ctx_exps, -1, keepdims=True) + jnp.sum(own_exps, -1, keepdims=True)
    return ctx_exps / total, own_exps / total


def shards(doc_states, context, gain, w_query, w_key, w_value, w_out, partners):
    tok, feat = doc_states.shape
    docs = tok // DOC_LEN
    width = w_query.shape[0]
    co_id = lax.axis_index("co")
    chip_id = lax.axis_index(("zl", "y"))
    dp_id = lax.axis_index(DP)

    swap = [(c * 16 + d, d * 16 + c) for c in range(16) for d in range(16)]
    own_ctx = wide(context)
    own_ctx_inv = inverse_rms(own_ctx)
    own_ctx_normed = (own_ctx * own_ctx_inv * gain).astype(bf16)
    named_rows = lax.ppermute(own_ctx_normed, EVERY, swap)
    few = jnp.concatenate([dot(named_rows, w_key), dot(named_rows, w_value)], axis=1).astype(bf16)
    few = ring(pair(pair(few, "co"), "zl"), "y")
    few = few.transpose(1, 0, 2, 3, 4).reshape(-1, 2 * HD)
    ctx_keys, ctx_values = few[:, :HD], few[:, HD:]

    by_zh = lax.all_gather(doc_states, "zh")
    rows = spread(by_zh, "x", 4).transpose(2, 1, 0, 3).reshape(tok, width)
    rows_wide = wide(rows)
    doc_inv = inverse_rms(rows_wide)
    normed = (rows_wide * doc_inv * gain).astype(bf16)
    queries = dot(normed, w_query).astype(bf16)
    doc_keys = dot(normed, w_key).astype(bf16)
    doc_values = dot(normed, w_value).astype(bf16)
    everyones = jnp.concatenate([queries, doc_keys, doc_values], axis=1)
    everyones = ring(pair(everyones, "zl"), "y")

    own_q, own_k, own_v = (a.reshape(docs, DOC_LEN, HD) for a in (queries, doc_keys, doc_values))
    ctx_probs, own_probs = probabilities(own_q, own_k, ctx_keys)
    mixture = ein("blc,ce->ble", ctx_probs.astype(bf16), ctx_values)
    mixture = mixture + ein("blm,bme->ble", own_probs.astype(bf16), own_v)
    averaging = (jnp.arange(tok)[None, :] // DOC_LEN == jnp.arange(docs)[:, None]).astype(bf16)
    averaging = averaging * jnp.asarray(1 / DOC_LEN, bf16)
    mean_mixture = dot(averaging, mixture.astype(bf16).reshape(tok, HD))
    branch = split_dot(mean_mixture, w_out, 3)
    branch = jnp.sum(spread(branch, "x", 4), axis=0)
    branch = jnp.sum(spread(branch, "zh", 4), axis=0)
    pooled = dot(averaging, rows) + branch

    extra = jnp.concatenate([doc_inv.reshape(docs, DOC_LEN), wide(partners)[:, None]], axis=1)
    extra = jnp.pad(extra, ((0, 0), (0, HD - extra.shape[1])))
    message = jnp.concatenate([pooled, mean_mixture, extra], axis=1)
    message = pair(spread(message, ("zl", "y"), 8), "co")
    side = 8 * docs
    total = 2 * side
    message = message.reshape(total, -1)
    pooled = message[:, :width]
    mean_mixture = message[:, width : width + HD]
    doc_inv = message[:, width + HD : width + HD + DOC_LEN]
    partners = message[:, width + HD + DOC_LEN].astype(jnp.int32)
    place = jnp.arange(total, dtype=jnp.int32)
    ids = ((place % side) // docs * 2 + place // side) * docs + place % docs

    length = jnp.sqrt(jnp.sum(pooled * pooled, axis=1) + 1e-06)
    unit = pooled / length[:, None]
    gram = jnp.dot(pooled, pooled.T, precision=EXACT)
    scores = gram / (length[:, None] * length[None, :]) / TEMPERATURE
    exps = jnp.where(ids[:, None] != ids[None, :], jnp.exp(scores), 0.0)
    sums = jnp.sum(exps, axis=1)
    chosen = (partners[:, None] == ids[None, :]).astype(f32)
    loss = jnp.mean(jnp.log(sums) - jnp.sum(scores * chosen, axis=1))
    coeff = (exps / sums[:, None] - chosen) / total * LOSS_SCALE
    grad_unit = jnp.dot(coeff + coeff.T, unit, precision=EXACT) / TEMPERATURE
    radial = jnp.sum(unit * grad_unit, axis=1, keepdims=True)
    grad_pooled = (grad_unit - unit * radial) / length[:, None]
    grad_part = lax.dynamic_slice_in_dim(grad_pooled, dp_id * feat, feat, 1)
    grad_out = jnp.dot(mean_mixture.T, grad_part, precision=EXACT)
    grad_side = lax.dynamic_slice_in_dim(grad_pooled, co_id * side, side, 0)
    grad_mixture = split_dot(grad_side / DOC_LEN, w_out.T, 3).astype(bf16)
    doc_inv = lax.dynamic_slice_in_dim(doc_inv, co_id * side, side, 0)

    factor = HD**-0.5
    everyones = everyones.transpose(1, 0, 2, 3).reshape(side * DOC_LEN, 3 * HD)
    all_q, all_k, all_v = (
        everyones[:, i * HD : (i + 1) * HD].reshape(side, DOC_LEN, HD) for i in range(3)
    )
    ctx_probs, own_probs = probabilities(all_q, all_k, ctx_keys)
    ctx_dweights = ein("be,ce->bc", grad_mixture, ctx_values)[:, None, :]
    own_dweights = ein("be,bme->bm", grad_mixture, all_v)[:, None, :]
    inner = jnp.sum(ctx_probs * ctx_dweights, -1, keepdims=True)
    inner = inner + jnp.sum(own_probs * own_dweights, -1, keepdims=True)
    ctx_dscores = (ctx_probs * (ctx_dweights - inner) * factor).astype(bf16)
    own_dscores = (own_probs * (own_dweights - inner) * factor).astype(bf16)
    own_weights = jnp.sum(wide(own_probs.astype(bf16)), axis=1)
    ctx_weights = jnp.sum(wide(ctx_probs.astype(bf16)), axis=1)
    grad_ctx_keys = ein("blc,ble->ce", ctx_dscores, all_q)
    grad_ctx_values = jnp.dot(ctx_weights.T, wide(grad_mixture), precision=EXACT)
    grad_ctx = jnp.concatenate([grad_ctx_keys, grad_ctx_values], axis=1)
    grad_ctx = grad_ctx + other_of_two(grad_ctx, "co")
    grad_queries = ein("blc,ce->ble", ctx_dscores, ctx_keys)
    grad_queries = (grad_queries + ein("blm,bme->ble", own_dscores, all_k)).astype(bf16)
    grad_keys = ein("blm,ble->bme", own_dscores, all_q).astype(bf16)
    grad_values = (own_weights[:, :, None] * wide(grad_mixture)[:, None, :]).astype(bf16)

    half = width // 2
    key_half = lax.dynamic_slice_in_dim(w_key, co_id * half, half, 0)
    value_half = lax.dynamic_slice_in_dim(w_value, co_id * half, half, 0)
    part = split_dot(grad_ctx[:, :HD], key_half.T, 2) + split_dot(grad_ctx[:, HD:], value_half.T, 2)
    part = lax.all_to_all(part.astype(bf16).reshape(16, -1, half), CTX, 0, 0)
    part = pair(jnp.sum(wide(part), axis=0), "co")
    scaled = gain * part.transpose(1, 0, 2).reshape(-1, width)
    grad_context = own_ctx_inv * scaled - own_ctx * own_ctx_inv**3 * jnp.mean(
        own_ctx * scaled, axis=1, keepdims=True
    )

    turn = [
        (((cy * 2 + s) * 16 + dy * 2 + k), ((dy * 2 + s) * 16 + cy * 2 + k))
        for cy in range(8)
        for dy in range(8)
        for s in range(2)
        for k in range(2)
    ]
    columns = lax.ppermute(doc_states, EVERY, turn)
    ctx_part = lax.dynamic_slice_in_dim(own_ctx_normed, dp_id * feat, feat, 1)
    columns = jnp.concatenate([columns, ctx_part], axis=0)
    columns, branch = lax.optimization_barrier((columns, branch))
    columns = ring(ring(columns, "zh"), "x").transpose(1, 0, 2, 3).reshape(16, -1, feat)
    ctx_columns = columns[:, tok:].reshape(-1, feat)
    gain_part = lax.dynamic_slice_in_dim(gain, chip_id * 2 * feat, 2 * feat, 0)
    columns = wide(columns[:, :tok]).reshape(8, 2, tok, feat) * doc_inv.reshape(8, 1, tok, 1)
    columns = (columns * gain_part.reshape(1, 2, 1, feat)).astype(bf16)
    columns = columns.transpose(0, 2, 1, 3).reshape(8 * tok, 2 * feat)
    grads = jnp.concatenate([grad_queries, grad_keys, grad_values], axis=2)
    grads = dot(columns.T, grads.reshape(8 * tok, 3 * HD)).reshape(2, feat, 3 * HD)
    mine = lax.dynamic_index_in_dim(grads, co_id, 0, keepdims=False)
    theirs = lax.dynamic_index_in_dim(grads, 1 - co_id, 0, keepdims=False)
    grads = mine + other_of_two(theirs, "co")
    from_ctx = split_dot(grad_ctx.T, ctx_columns, 2).T
    grad_query = grads[:, :HD]
    grad_key = grads[:, HD : 2 * HD] + from_ctx[:, :HD]
    grad_value = grads[:, 2 * HD :] + from_ctx[:, HD:]
    return loss, grad_context, grad_query, grad_key, grad_value, grad_out


def solution(mesh):
    split = Mesh(mesh.devices.reshape(4, 4, 2, 4, 2), EVERY)
    in_specs = (
        P(DP, CTX),
        P(CTX, None),
        P(),
        P(None, CTX),
        P(None, CTX),
        P(None, CTX),
        P(CTX, None),
        P(DP),
    )
    out_specs = (P(), P(CTX, None), P(DP, CTX), P(DP, CTX), P(DP, CTX), P(CTX, DP))
    return jax.shard_map(
        shards, mesh=split, in_specs=in_specs, out_specs=out_specs, check_vma=False
    )
```

time: 230 us -> 234 us (1.017)
  the two profiles are of different devices: /device:TPU:1 before, /device:TPU:41 now
where the time goes in v3:
time: 234 us; the launch traced here: 233 us
  starting transfers between devices  66.3 us (28%)
  waiting for transfers between devices  51.4 us (22%)
  local copies, waits for them, and re-layouts  43.8 us (19%)
  other arithmetic  26.1 us (11%)
  matrix products  25.6 us (11%)
  blocking collectives  16.3 us (7%)
  between operations  3.33 us (1%)
    ppermute x12, waiting for transfers between devices, ring(): lax.ppermute(a, axis, [(i, (i + k) % 4) for i in range(4)])  24.7 us
    all_to_all x4, starting transfers between devices, spread(): return lax.all_to_all(copies, axis, 0, 0)  21.8 us
    unnamed x114, local copies, waits for them, and re-layouts  21.3 us
    ppermute x12, starting transfers between devices, ring(): lax.ppermute(a, axis, [(i, (i + k) % 4) for i in range(4)])  18.9 us
    all_gather x1, blocking collectives, shards(): by_zh = lax.all_gather(doc_states, 'zh')  16.3 us
    all_to_all x4, waiting for transfers between devices, spread(): return lax.all_to_all(copies, axis, 0, 0)  11.7 us
    dot_general x12, matrix products, ein(): return jnp.einsum(form, a, b, preferred_element_type=f32)  11.1 us
    dot_general x13, matrix products, dot(): return jnp.dot(a, b, preferred_element_type=f32)  10.1 us
  transfers between devices with their start and end apart: 26, of which 10 were waited for; matrix products, arithmetic and copies ran while one was open for 29% of the time, Pallas kernels for 0%

profile of v3, /device:TPU:41, one launch (start us, length us, event | category | flops | bytes accessed | tf_op | source)
XLA Modules:
  0.0 232.8 jit_solution(15131141100092062100)
XLA Ops:
  0.6 1.1 fusion.30
  2.3 0.9 fusion.32
  3.2 10.1 %collective-permute-start = (bf16[8,4096]{1,0:T(8,128)(2,1)S(1)}, bf16[8,4096]{1,0:T(8,128)(2,1)S(1)}, u32[]{:S(2)}, u32[]{:S(2)}) collective-permute-start(bf16[8,4096]{1,0:T(8,128)(2,1)S(1)} %fusion.32), channel_id=1, source_target_pairs={{0,0},{1,16},{2,32},{3,48},{4,64},{5,80},{6,96},{7,112},{8,128},{9... | collective-permute-start | bytes 196616 | tf_op jit(solution)/shard_map/ppermute | solution.py:95
  13.4 2.1 collective-permute-start.13
  15.4 16.3 %all-gather = bf16[1024,256]{1,0:T(8,128)(2,1)S(1)} all-gather(bf16[256,256]{1,0:T(8,128)(2,1)} %param.8), channel_id=2, replica_groups=mesh['zh'=4,'x'=4,'zl'=2,'y'=4,'co'=2] {'zh'}, dimensions={0}, use_global_device_ids=true | all-gather | bytes 655360 | tf_op jit(solution)/shard_map/all_gather | solution.py:101
  31.9 1.6 broadcast_in_dim.13
  33.5 6.9 %all-to-all-start = ((bf16[4,4,256,256]{2,3,1,0:T(8,128)(2,1)}), bf16[4,4,256,256]{2,3,1,0:T(8,128)(2,1)S(1)}, u32[]{:S(2)}, u32[]{:S(2)}) async-start(bf16[4,4,256,256]{2,3,1,0:T(8,128)(2,1)} %broadcast_in_dim.13), calls=%async_computation | async-start | bytes 4194304 | tf_op jit(solution)/shard_map/all_to_all | solution.py:55
  41.5 1.5 convolution_convert_fusion.4
  43.2 2.4 %collective-permute-start.1 = (bf16[8,256]{1,0:T(8,128)(2,1)S(1)}, bf16[8,256]{1,0:T(8,128)(2,1)S(1)}, u32[]{:S(2)}, u32[]{:S(2)}) collective-permute-start(bf16[8,256]{1,0:T(8,128)(2,1)S(1)} %pad_maximum_fusion.5), channel_id=1, source_target_pairs={{0,1},{1,0},{2,3},{3,2},{4,5},{5,4},{6,7},{7,6},{8,9},{9,8},{10,11... | collective-permute-start | bytes 12296 | tf_op jit(solution)/shard_map/ppermute | solution.py:59
  46.6 2.6 %collective-permute-done.2 = bf16[2,8,256]{2,1,0:T(8,128)(2,1)S(1)} collective-permute-done((bf16[2,8,256]{2,1,0:T(8,128)(2,1)S(1)}, bf16[2,8,256]{2,1,0:T(8,128)(2,1)S(1)}, u32[]{:S(2)}, u32[]{:S(2)}) %collective-permute-start.2) | collective-permute-done | bytes 8224 | tf_op jit(solution)/shard_map/ppermute | solution.py:59
  49.2 0.9 collective-permute-start.3
  50.7 2.9 %collective-permute-start.4 = (bf16[2,2,8,256]{3,2,1,0:T(8,128)(2,1)S(1)}, bf16[2,2,8,256]{3,2,1,0:T(8,128)(2,1)S(1)}, u32[]{:S(2)}, u32[]{:S(2)}) collective-permute-start(bf16[2,2,8,256]{3,2,1,0:T(8,128)(2,1)S(1)} %maximum_select_fusion.4), channel_id=1, source_target_pairs={{0,4},{2,6},{4,0},{6,2},{1,5},{3,7},{5,1},{7,3},{8,12},{10,14},{12... | collective-permute-start | bytes 49160 | tf_op jit(solution)/shard_map/ppermute | solution.py:69
  53.6 1.5 collective-permute-done.4
  55.2 9.3 %all-to-all-done = bf16[4,4,256,256]{2,3,1,0:T(8,128)(2,1)S(1)} async-done(((bf16[4,4,256,256]{2,3,1,0:T(8,128)(2,1)}), bf16[4,4,256,256]{2,3,1,0:T(8,128)(2,1)S(1)}, u32[]{:S(2)}, u32[]{:S(2)}) %all-to-all-start) | async-done | bytes 2097184 | tf_op jit(solution)/shard_map/all_to_all | solution.py:55
  65.9 1.7 copy.73
  74.3 3.4 %all-to-all-start.1 = ((f32[4,4,4096]{2,1,0:T(4,128)}), f32[4,4,4096]{2,1,0:T(4,128)S(1)}, u32[]{:S(2)}, u32[]{:S(2)}) async-start(f32[4,4,4096]{2,1,0:T(4,128)} %broadcast_in_dim.14), calls=%async_computation.1 | async-start | bytes 524288 | tf_op jit(solution)/shard_map/all_to_all | solution.py:55
  78.9 1.3 copy.76
  80.9 2.4 %all-to-all-done.1 = f32[4,4,4096]{2,1,0:T(4,128)S(1)} async-done(((f32[4,4,4096]{2,1,0:T(4,128)}), f32[4,4,4096]{2,1,0:T(4,128)S(1)}, u32[]{:S(2)}, u32[]{:S(2)}) %all-to-all-start.1) | async-done | bytes 262176 | tf_op jit(solution)/shard_map/all_to_all | solution.py:55
  84.0 5.4 %all-to-all-start.2 = ((f32[4,4,4096]{2,1,0:T(4,128)}), f32[4,4,4096]{2,1,0:T(4,128)}, u32[]{:S(2)}, u32[]{:S(2)}) async-start(f32[4,4,4096]{2,1,0:T(4,128)} %broadcast_in_dim.15), calls=%async_computation.2 | async-start | bytes 524288 | tf_op jit(solution)/shard_map/all_to_all | solution.py:55
  89.5 1.7 fusion.135
  92.0 1.6 pad_maximum_fusion.2
  93.6 1.3 rsqrt.25
  94.8 1.3 select_maximum_fusion
  96.2 3.5 %collective-permute-done.7 = bf16[256,384]{1,0:T(8,128)(2,1)S(1)} collective-permute-done((bf16[256,384]{1,0:T(8,128)(2,1)}, bf16[256,384]{1,0:T(8,128)(2,1)S(1)}, u32[]{:S(2)}, u32[]{:S(2)}) %collective-permute-start.7) | collective-permute-done | bytes 196640 | tf_op jit(solution)/shard_map/ppermute | solution.py:59
  101.5 1.2 collective-permute-start.9
  103.5 1.6 reduce_sum.176
  105.1 2.1 collective-permute-start.16
  107.2 2.9 %collective-permute-start.15 = (bf16[264,256]{1,0:T(8,128)(2,1)}, bf16[264,256]{1,0:T(8,128)(2,1)}, u32[]{:S(2)}, u32[]{:S(2)}) collective-permute-start(bf16[264,256]{1,0:T(8,128)(2,1)} %pad_maximum_fusion.2), channel_id=1, source_target_pairs={{0,128},{64,192},{128,0},{192,64},{1,129},{65,193},{129,1},{193,65... | collective-permute-start | bytes 405512 | tf_op jit(solution)/shard_map/ppermute | solution.py:69
  110.1 1.5 convolution_add_fusion
  112.5 6.1 %all-to-all-start.3 = ((f32[8,4,4352]{2,1,0:T(4,128)}), f32[8,4,4352]{2,1,0:T(4,128)S(1)}, u32[]{:S(2)}, u32[]{:S(2)}) async-start(f32[8,4,4352]{2,1,0:T(4,128)} %broadcast_in_dim.17), calls=%async_computation.3 | async-start | bytes 1114112 | tf_op jit(solution)/shard_map/all_to_all | solution.py:55
  118.6 3.5 %collective-permute-done.8 = bf16[2,256,384]{2,1,0:T(8,128)(2,1)} collective-permute-done((bf16[2,256,384]{2,1,0:T(8,128)(2,1)}, bf16[2,256,384]{2,1,0:T(8,128)(2,1)}, u32[]{:S(2)}, u32[]{:S(2)}) %collective-permute-start.8) | collective-permute-done | bytes 393248 | tf_op jit(solution)/shard_map/ppermute | solution.py:69
  122.1 4.2 %collective-permute-start.14 = (bf16[264,256]{1,0:T(8,128)(2,1)}, bf16[264,256]{1,0:T(8,128)(2,1)S(1)}, u32[]{:S(2)}, u32[]{:S(2)}) collective-permute-start(bf16[264,256]{1,0:T(8,128)(2,1)} %pad_maximum_fusion.2), channel_id=1, source_target_pairs={{0,192},{64,0},{128,64},{192,128},{1,193},{65,1},{129,65},{193,129... | collective-permute-start | bytes 405512 | tf_op jit(solution)/shard_map/ppermute | solution.py:69
  126.3 1.0 bitcast_dynamic-update-slice_fusion.11
  127.3 1.1 bitcast_dynamic-update-slice_fusion.9
  128.6 1.1 bitcast_dynamic-update-slice_fusion.12
  129.7 1.1 bitcast_dynamic-update-slice_fusion.10
  131.2 1.1 fusion.140
  132.3 1.1 bitcast_dynamic-update-slice_fusion.16
  136.3 1.7 collective-permute-start.18
  137.9 1.1 collective-permute-start.17
  139.0 1.4 fusion.143
  140.8 1.4 fusion.144
  142.2 18.9 %collective-permute-done.17 = bf16[4,264,256]{2,1,0:T(8,128)(2,1)S(1)} collective-permute-done((bf16[4,264,256]{2,1,0:T(8,128)(2,1)S(1)}, bf16[4,264,256]{2,1,0:T(8,128)(2,1)S(1)}, u32[]{:S(2)}, u32[]{:S(2)}) %collective-permute-start.17) | collective-permute-done | bytes 540704 | tf_op jit(solution)/shard_map/ppermute | solution.py:69
  168.6 1.7 constant_dynamic-slice_fusion.1
  170.4 1.7 slice.139
  172.4 1.3 maximum_select_fusion
  173.7 1.6 select_n.228
  175.8 1.0 fusion.11
  177.6 1.3 multiply_reduce_fusion.3
  183.6 1.8 fusion.54
  185.4 1.3 convolution_convert_fusion
  187.0 3.0 %fusion.5 = bf16[32,64,128]{2,1,0:T(8,128)(2,1)} fusion(f32[32,64,128]{2,1,0:T(8,128)} %fusion.54, bf16[32,64,128]{2,1,0:T(8,128)(2,1)S(1)} %bitcast.191, f32[32,64]{1,0:T(8,128)S(1)} %add.274, f32[32,64]{1,0:T(8,128)S(1)} %bitcast.223, f32[32,64,64]{1,2,0:T(8,128)S(1)} %copy-done.8, f32[32,64]{1,0:T(8,128)S(1)} %add.269), kind=kOutput, calls=%fused_computation.16 | convolution fusion | flops 34734080 | bytes 2646016 | tf_op jit(solution)/shard_map/blm,bme->ble/dot_general | solution.py:46
  191.2 3.1 %copy.83 = bf16[8,256,2,256]{1,0,3,2:T(8,128)(2,1)} copy(bf16[8,256,2,256]{3,1,2,0:T(8,128)(2,1)S(1)} %fusion.2) | data formatting | bytes 4194304 | tf_op jit(solution)/shard_map/transpose | solution.py:206
  194.3 2.4 %copy.94 = bf16[64,8,8,256]{3,1,2,0:T(8,128)(2,1)S(1)} copy(bf16[64,8,8,256]{3,2,1,0:T(8,128)(2,1)} %bitcast.181) | data formatting | bytes 4194304
  197.3 1.3 fusion.146
  198.6 1.6 reduce-precision_convert_fusion.2
  201.9 1.1 fusion.21
  202.9 7.5 %all-to-all-start.4 = ((bf16[16,8,2048]{2,1,0:T(8,128)(2,1)}), bf16[16,8,2048]{2,1,0:T(8,128)(2,1)S(1)}, u32[]{:S(2)}, u32[]{:S(2)}) async-start(bf16[16,8,2048]{2,1,0:T(8,128)(2,1)} %fusion.21), calls=%async_computation.4 | async-start | bytes 1048576 | tf_op jit(solution)/shard_map/all_to_all | solution.py:183
  210.5 1.3 subtract_reduce_fusion
  214.4 1.8 fusion.50
  217.1 1.0 fusion.36
  218.3 1.0 add.290
  219.3 8.0 %all-to-all-done.4 = bf16[16,8,2048]{2,1,0:T(8,128)(2,1)S(1)} async-done(((bf16[16,8,2048]{2,1,0:T(8,128)(2,1)}), bf16[16,8,2048]{2,1,0:T(8,128)(2,1)S(1)}, u32[]{:S(2)}, u32[]{:S(2)}) %all-to-all-start.4) | async-done | bytes 524320 | tf_op jit(solution)/shard_map/all_to_all | solution.py:183
  227.4 0.9 collective-permute-start.12
  (220 shorter events, 46.1 us)
Async XLA Ops:
  0.6 42.3 %copy-start = (bf16[4096,128]{1,0:T(8,128)(2,1)S(1)}, bf16[4096,128]{1,0:T(8,128)(2,1)}, u32[]{:S(2)}) copy-start(bf16[4096,128]{1,0:T(8,128)(2,1)} %param.12) | copy-start | bytes 3145732
  2.3 29.4 %copy-start.38 = (f32[8]{0:T(128)}, f32[8]{0:T(128)S(1)}, u32[]{:S(2)}) copy-start(f32[8]{0:T(128)S(1)} %get-tuple-element.70) | copy-start | bytes 100
  3.2 38.3 %collective-permute-start = (bf16[8,4096]{1,0:T(8,128)(2,1)S(1)}, bf16[8,4096]{1,0:T(8,128)(2,1)S(1)}, u32[]{:S(2)}, u32[]{:S(2)}) collective-permute-start(bf16[8,4096]{1,0:T(8,128)(2,1)S(1)} %fusion.32), channel_id=1, source_target_pairs={{0,0},{1,16},{2,32},{3,48},{4,64},{5,80},{6,96},{7,112},{8,128},{9... | collective-permute-start | bytes 196616 | tf_op jit(solution)/shard_map/ppermute | solution.py:95
  13.4 78.6 %collective-permute-start.13 = (bf16[256,256]{1,0:T(8,128)(2,1)}, bf16[256,256]{1,0:T(8,128)(2,1)}, u32[]{:S(2)}, u32[]{:S(2)}) collective-permute-start(bf16[256,256]{1,0:T(8,128)(2,1)} %param.8), channel_id=1, source_target_pairs={{0,0},{1,1},{16,16},{17,17},{2,32},{3,33},{18,48},{19,49},{4,64},{... | collective-permute-start | bytes 393224 | tf_op jit(solution)/shard_map/ppermute | solution.py:197
  33.5 6.9 %copy-start.43 = (s32[4]{0:T(128)S(1)}, s32[4]{0:T(128)}, u32[]{:S(2)}) copy-start(s32[4]{0:T(128)} %param.15) | copy-start | bytes 52
  33.5 31.0 %all-to-all-start = ((bf16[4,4,256,256]{2,3,1,0:T(8,128)(2,1)}), bf16[4,4,256,256]{2,3,1,0:T(8,128)(2,1)S(1)}, u32[]{:S(2)}, u32[]{:S(2)}) async-start(bf16[4,4,256,256]{2,3,1,0:T(8,128)(2,1)} %broadcast_in_dim.13), calls=%async_computation | async-start | bytes 4194304 | tf_op jit(solution)/shard_map/all_to_all | solution.py:55
  43.2 3.2 %collective-permute-start.1 = (bf16[8,256]{1,0:T(8,128)(2,1)S(1)}, bf16[8,256]{1,0:T(8,128)(2,1)S(1)}, u32[]{:S(2)}, u32[]{:S(2)}) collective-permute-start(bf16[8,256]{1,0:T(8,128)(2,1)S(1)} %pad_maximum_fusion.5), channel_id=1, source_target_pairs={{0,1},{1,0},{2,3},{3,2},{4,5},{5,4},{6,7},{7,6},{8,9},{9,8},{10,11... | collective-permute-start | bytes 12296 | tf_op jit(solution)/shard_map/ppermute | solution.py:59
  46.4 2.8 %collective-permute-start.2 = (bf16[2,8,256]{2,1,0:T(8,128)(2,1)S(1)}, bf16[2,8,256]{2,1,0:T(8,128)(2,1)S(1)}, u32[]{:S(2)}, u32[]{:S(2)}) collective-permute-start(bf16[2,8,256]{2,1,0:T(8,128)(2,1)S(1)} %maximum_select_fusion.7), channel_id=1, source_target_pairs={{0,8},{8,0},{1,9},{9,1},{2,10},{10,2},{3,11},{11,3},{4,12},{12,4},... | collective-permute-start | bytes 24584 | tf_op jit(solution)/shard_map/ppermute | solution.py:59
  49.2 4.4 %collective-permute-start.3 = (bf16[2,2,8,256]{3,2,1,0:T(8,128)(2,1)S(1)}, bf16[2,2,8,256]{3,2,1,0:T(8,128)(2,1)S(1)}, u32[]{:S(2)}, u32[]{:S(2)}) collective-permute-start(bf16[2,2,8,256]{3,2,1,0:T(8,128)(2,1)S(1)} %maximum_select_fusion.4), channel_id=1, source_target_pairs={{0,6},{2,0},{4,2},{6,4},{1,7},{3,1},{5,3},{7,5},{8,14},{10,8},{12,... | collective-permute-start | bytes 49160 | tf_op jit(solution)/shard_map/ppermute | solution.py:69
  50.2 4.9 %collective-permute-start.5 = (bf16[2,2,8,256]{3,2,1,0:T(8,128)(2,1)S(1)}, bf16[2,2,8,256]{3,2,1,0:T(8,128)(2,1)S(1)}, u32[]{:S(2)}, u32[]{:S(2)}) collective-permute-start(bf16[2,2,8,256]{3,2,1,0:T(8,128)(2,1)S(1)} %maximum_select_fusion.4), channel_id=1, source_target_pairs={{0,2},{2,4},{4,6},{6,0},{1,3},{3,5},{5,7},{7,1},{8,10},{10,12},{12... | collective-permute-start | bytes 49160 | tf_op jit(solution)/shard_map/ppermute | solution.py:69
  50.7 4.4 %collective-permute-start.4 = (bf16[2,2,8,256]{3,2,1,0:T(8,128)(2,1)S(1)}, bf16[2,2,8,256]{3,2,1,0:T(8,128)(2,1)S(1)}, u32[]{:S(2)}, u32[]{:S(2)}) collective-permute-start(bf16[2,2,8,256]{3,2,1,0:T(8,128)(2,1)S(1)} %maximum_select_fusion.4), channel_id=1, source_target_pairs={{0,4},{2,6},{4,0},{6,2},{1,5},{3,7},{5,1},{7,3},{8,12},{10,14},{12... | collective-permute-start | bytes 49160 | tf_op jit(solution)/shard_map/ppermute | solution.py:69
  55.2 16.9 %copy-start.26 = (bf16[2,4,2,8,256]{4,3,2,1,0:T(8,128)(2,1)}, bf16[2,4,2,8,256]{4,3,2,1,0:T(8,128)(2,1)S(1)}, u32[]{:S(2)}) copy-start(bf16[2,4,2,8,256]{4,3,2,1,0:T(8,128)(2,1)S(1)} %copy.74) | copy-start | bytes 196612
  64.5 1.3 copy-start.1
  65.9 1.8 copy-start.33
  65.9 1.8 copy-start.28
  69.6 2.8 %copy-start.29 = (bf16[256,128]{1,0:T(8,128)(2,1)}, bf16[256,128]{1,0:T(8,128)(2,1)S(1)}, u32[]{:S(2)}) copy-start(bf16[256,128]{1,0:T(8,128)(2,1)S(1)} %convolution_convert_fusion.1) | copy-start | bytes 196612
  70.9 1.5 copy-start.21
  70.9 1.7 copy-start.37
  70.9 2.4 %copy-start.15 = (bf16[128,4096]{1,0:T(8,128)(2,1)S(1)}, bf16[128,4096]{1,0:T(8,128)(2,1)}, u32[]{:S(2)}) copy-start(bf16[128,4096]{1,0:T(8,128)(2,1)} %param.14) | copy-start | bytes 3145732
  74.3 8.9 %all-to-all-start.1 = ((f32[4,4,4096]{2,1,0:T(4,128)}), f32[4,4,4096]{2,1,0:T(4,128)S(1)}, u32[]{:S(2)}, u32[]{:S(2)}) async-start(f32[4,4,4096]{2,1,0:T(4,128)} %broadcast_in_dim.14), calls=%async_computation.1 | async-start | bytes 524288 | tf_op jit(solution)/shard_map/all_to_all | solution.py:55
  84.0 19.5 %all-to-all-start.2 = ((f32[4,4,4096]{2,1,0:T(4,128)}), f32[4,4,4096]{2,1,0:T(4,128)}, u32[]{:S(2)}, u32[]{:S(2)}) async-start(f32[4,4,4096]{2,1,0:T(4,128)} %broadcast_in_dim.15), calls=%async_computation.2 | async-start | bytes 524288 | tf_op jit(solution)/shard_map/all_to_all | solution.py:55
  91.1 8.6 %collective-permute-start.7 = (bf16[256,384]{1,0:T(8,128)(2,1)}, bf16[256,384]{1,0:T(8,128)(2,1)S(1)}, u32[]{:S(2)}, u32[]{:S(2)}) collective-permute-start(bf16[256,384]{1,0:T(8,128)(2,1)} %get-tuple-element.61), channel_id=1, source_target_pairs={{0,8},{8,0},{1,9},{9,1},{2,10},{10,2},{3,11},{11,3},{4,12},{12,4},... | collective-permute-start | bytes 589832 | tf_op jit(solution)/shard_map/ppermute | solution.py:59
  101.2 27.2 %collective-permute-start.10 = (bf16[2,256,384]{2,1,0:T(8,128)(2,1)}, bf16[2,256,384]{2,1,0:T(8,128)(2,1)S(1)}, u32[]{:S(2)}, u32[]{:S(2)}) collective-permute-start(bf16[2,256,384]{2,1,0:T(8,128)(2,1)} %maximum_select_fusion.1), channel_id=1, source_target_pairs={{0,2},{2,4},{4,6},{6,0},{1,3},{3,5},{5,7},{7,1},{8,10},{10,12},{12... | collective-permute-start | bytes 1179656 | tf_op jit(solution)/shard_map/ppermute | solution.py:69
  101.5 25.8 %collective-permute-start.9 = (bf16[2,256,384]{2,1,0:T(8,128)(2,1)}, bf16[2,256,384]{2,1,0:T(8,128)(2,1)}, u32[]{:S(2)}, u32[]{:S(2)}) collective-permute-start(bf16[2,256,384]{2,1,0:T(8,128)(2,1)} %maximum_select_fusion.1), channel_id=1, source_target_pairs={{0,4},{2,6},{4,0},{6,2},{1,5},{3,7},{5,1},{7,3},{8,12},{10,14},{12... | collective-permute-start | bytes 1179656 | tf_op jit(solution)/shard_map/ppermute | solution.py:69
  102.7 19.4 %collective-permute-start.8 = (bf16[2,256,384]{2,1,0:T(8,128)(2,1)}, bf16[2,256,384]{2,1,0:T(8,128)(2,1)}, u32[]{:S(2)}, u32[]{:S(2)}) collective-permute-start(bf16[2,256,384]{2,1,0:T(8,128)(2,1)} %maximum_select_fusion.1), channel_id=1, source_target_pairs={{0,6},{2,0},{4,2},{6,4},{1,7},{3,1},{5,3},{7,5},{8,14},{10,8},{12,... | collective-permute-start | bytes 1179656 | tf_op jit(solution)/shard_map/ppermute | solution.py:69
  105.1 6.4 %copy-start.34 = (f32[4,128]{1,0:T(4,128)S(1)}, f32[4,128]{1,0:T(4,128)}, u32[]{:S(2)}) copy-start(f32[4,128]{1,0:T(4,128)} %get-tuple-element.75) | copy-start | bytes 6148
  105.1 6.4 %copy-start.35 = (f32[4,128]{1,0:T(4,128)S(1)}, f32[4,128]{1,0:T(4,128)}, u32[]{:S(2)}) copy-start(f32[4,128]{1,0:T(4,128)} %select_maximum_fusion) | copy-start | bytes 6148
  105.1 28.2 %collective-permute-start.16 = (bf16[264,256]{1,0:T(8,128)(2,1)}, bf16[264,256]{1,0:T(8,128)(2,1)}, u32[]{:S(2)}, u32[]{:S(2)}) collective-permute-start(bf16[264,256]{1,0:T(8,128)(2,1)} %pad_maximum_fusion.2), channel_id=1, source_target_pairs={{0,64},{64,128},{128,192},{192,0},{1,65},{65,129},{129,193},{193,1... | collective-permute-start | bytes 405512 | tf_op jit(solution)/shard_map/ppermute | solution.py:69
  107.2 25.0 %collective-permute-start.15 = (bf16[264,256]{1,0:T(8,128)(2,1)}, bf16[264,256]{1,0:T(8,128)(2,1)}, u32[]{:S(2)}, u32[]{:S(2)}) collective-permute-start(bf16[264,256]{1,0:T(8,128)(2,1)} %pad_maximum_fusion.2), channel_id=1, source_target_pairs={{0,128},{64,192},{128,0},{192,64},{1,129},{65,193},{129,1},{193,65... | collective-permute-start | bytes 405512 | tf_op jit(solution)/shard_map/ppermute | solution.py:69
  111.6 16.9 %copy-start.18 = (bf16[1,1,256,384]{3,2,1,0:T(8,128)(2,1)S(1)}, bf16[1,1,256,384]{3,2,1,0:T(8,128)(2,1)}, u32[]{:S(2)}) copy-start(bf16[1,1,256,384]{3,2,1,0:T(8,128)(2,1)} %get-tuple-element.59) | copy-start | bytes 589828
  111.6 16.9 %copy-start.20 = (bf16[256,384]{1,0:T(8,128)(2,1)S(1)}, bf16[256,384]{1,0:T(8,128)(2,1)}, u32[]{:S(2)}) copy-start(bf16[256,384]{1,0:T(8,128)(2,1)} %copy-done.19) | copy-start | bytes 589828
  112.5 53.7 %all-to-all-start.3 = ((f32[8,4,4352]{2,1,0:T(4,128)}), f32[8,4,4352]{2,1,0:T(4,128)S(1)}, u32[]{:S(2)}, u32[]{:S(2)}) async-start(f32[8,4,4352]{2,1,0:T(4,128)} %broadcast_in_dim.17), calls=%async_computation.3 | async-start | bytes 1114112 | tf_op jit(solution)/shard_map/all_to_all | solution.py:55
  122.1 10.1 %collective-permute-start.14 = (bf16[264,256]{1,0:T(8,128)(2,1)}, bf16[264,256]{1,0:T(8,128)(2,1)S(1)}, u32[]{:S(2)}, u32[]{:S(2)}) collective-permute-start(bf16[264,256]{1,0:T(8,128)(2,1)} %pad_maximum_fusion.2), channel_id=1, source_target_pairs={{0,192},{64,0},{128,64},{192,128},{1,193},{65,1},{129,65},{193,129... | collective-permute-start | bytes 405512 | tf_op jit(solution)/shard_map/ppermute | solution.py:69
  131.2 3.2 %copy-start.22 = (bf16[264,256]{1,0:T(8,128)(2,1)S(1)}, bf16[264,256]{1,0:T(8,128)(2,1)}, u32[]{:S(2)}) copy-start(bf16[264,256]{1,0:T(8,128)(2,1)} %pad_maximum_fusion.2) | copy-start | bytes 405508
  132.2 8.5 %copy-start.11 = (bf16[2048,128]{1,0:T(8,128)(2,1)}, bf16[2048,128]{1,0:T(8,128)(2,1)S(1)}, u32[]{:S(2)}) copy-start(bf16[2048,128]{1,0:T(8,128)(2,1)S(1)} %get-tuple-element.49) | copy-start | bytes 1572868
  132.3 6.8 %copy-start.27 = (bf16[2,4,2,8,256]{4,3,2,1,0:T(8,128)(2,1)S(1)}, bf16[2,4,2,8,256]{4,3,2,1,0:T(8,128)(2,1)}, u32[]{:S(2)}) copy-start(bf16[2,4,2,8,256]{4,3,2,1,0:T(8,128)(2,1)} %copy-done.26) | copy-start | bytes 196612
  136.3 25.7 %collective-permute-start.18 = (bf16[4,264,256]{2,1,0:T(8,128)(2,1)S(1)}, bf16[4,264,256]{2,1,0:T(8,128)(2,1)S(1)}, u32[]{:S(2)}, u32[]{:S(2)}) collective-permute-start(bf16[4,264,256]{2,1,0:T(8,128)(2,1)S(1)} %constant_dynamic-slice_fusion.2), channel_id=1, source_target_pairs={{0,32},{16,48},{32,0},{48,16},{1,33},{17,49},{33,1},{49,17},{2,34}... | collective-permute-start | bytes 1622024 | tf_op jit(solution)/shard_map/ppermute | solution.py:69
  137.9 23.2 %collective-permute-start.17 = (bf16[4,264,256]{2,1,0:T(8,128)(2,1)S(1)}, bf16[4,264,256]{2,1,0:T(8,128)(2,1)S(1)}, u32[]{:S(2)}, u32[]{:S(2)}) collective-permute-start(bf16[4,264,256]{2,1,0:T(8,128)(2,1)S(1)} %constant_dynamic-slice_fusion.2), channel_id=1, source_target_pairs={{0,48},{16,0},{32,16},{48,32},{1,49},{17,1},{33,17},{49,33},{2,50}... | collective-permute-start | bytes 1622024 | tf_op jit(solution)/shard_map/ppermute | solution.py:69
  140.4 23.2 %collective-permute-start.19 = (bf16[4,264,256]{2,1,0:T(8,128)(2,1)S(1)}, bf16[4,264,256]{2,1,0:T(8,128)(2,1)S(1)}, u32[]{:S(2)}, u32[]{:S(2)}) collective-permute-start(bf16[4,264,256]{2,1,0:T(8,128)(2,1)S(1)} %constant_dynamic-slice_fusion.2), channel_id=1, source_target_pairs={{0,16},{16,32},{32,48},{48,0},{1,17},{17,33},{33,49},{49,1},{2,18}... | collective-permute-start | bytes 1622024 | tf_op jit(solution)/shard_map/ppermute | solution.py:69
  166.2 6.2 %collective-permute-start.6 = (f32[8,4,4352]{2,1,0:T(4,128)S(1)}, f32[8,4,4352]{2,1,0:T(4,128)S(1)}, u32[]{:S(2)}, u32[]{:S(2)}) collective-permute-start(f32[8,4,4352]{2,1,0:T(4,128)S(1)} %all-to-all-done.3), channel_id=1, source_target_pairs={{0,1},{1,0},{2,3},{3,2},{4,5},{5,4},{6,7},{7,6},{8,9},{9,8},{10,11... | collective-permute-start | bytes 1671176 | tf_op jit(solution)/shard_map/ppermute | solution.py:59
  170.4 2.0 copy-start.4
  173.7 3.1 %copy-start.40 = (s32[64]{0:T(128)S(1)}, s32[64]{0:T(128)}, u32[]{:S(2)}) copy-start(s32[64]{0:T(128)} %fusion.114) | copy-start | bytes 772
  175.4 3.5 %copy-start.2 = (f32[64,4352]{1,0:T(8,128)}, f32[64,4352]{1,0:T(8,128)S(1)}, u32[]{:S(2)}) copy-start(f32[64,4352]{1,0:T(8,128)S(1)} %select_n.228) | copy-start | bytes 3342340
  179.1 1.6 copy-start.10
  179.1 1.7 copy-start.23
  179.3 2.0 copy-start.8
  180.2 1.8 copy-start.9
  183.6 6.4 %copy-start.30 = (f32[128,128]{0,1:T(8,128)}, f32[128,128]{0,1:T(8,128)S(1)}, u32[]{:S(2)}) copy-start(f32[128,128]{0,1:T(8,128)S(1)} %convolution_bitcast_fusion) | copy-start | bytes 196612
  185.4 1.6 copy-start.12
  187.0 3.7 %copy-start.5 = (bf16[16,256,256]{2,1,0:T(8,128)(2,1)S(1)}, bf16[16,256,256]{2,1,0:T(8,128)(2,1)}, u32[]{:S(2)}) copy-start(bf16[16,256,256]{2,1,0:T(8,128)(2,1)} %slice.139) | copy-start | bytes 6291460
  187.0 3.6 %copy-start.36 = (f32[2,256]{1,0:T(2,128)S(1)}, f32[2,256]{1,0:T(2,128)}, u32[]{:S(2)}) copy-start(f32[2,256]{1,0:T(2,128)} %mul.306) | copy-start | bytes 6148
  190.6 8.0 %collective-permute-start.11 = (f32[128,256]{0,1:T(8,128)}, f32[128,256]{0,1:T(8,128)}, u32[]{:S(2)}, u32[]{:S(2)}) collective-permute-start(f32[128,256]{0,1:T(8,128)} %pad_maximum_fusion.3), channel_id=1, source_target_pairs={{0,1},{1,0},{2,3},{3,2},{4,5},{5,4},{6,7},{7,6},{8,9},{9,8},{10,11... | collective-permute-start | bytes 393224 | tf_op jit(solution)/shard_map/ppermute | solution.py:59
  194.3 2.7 %copy-start.24 = (bf16[32,64,128]{2,1,0:T(8,128)(2,1)S(1)}, bf16[32,64,128]{2,1,0:T(8,128)(2,1)}, u32[]{:S(2)}) copy-start(bf16[32,64,128]{2,1,0:T(8,128)(2,1)} %convolution_convert_fusion) | copy-start | bytes 1572868
  194.3 2.7 %copy-start.25 = (bf16[32,64,128]{2,1,0:T(8,128)(2,1)S(1)}, bf16[32,64,128]{2,1,0:T(8,128)(2,1)}, u32[]{:S(2)}) copy-start(bf16[32,64,128]{2,1,0:T(8,128)(2,1)} %fusion.5) | copy-start | bytes 1572868
  197.3 1.4 copy-start.31
  198.6 2.8 %copy-start.7 = (bf16[4096,128]{1,0:T(8,128)(2,1)S(1)}, bf16[4096,128]{1,0:T(8,128)(2,1)}, u32[]{:S(2)}) copy-start(bf16[4096,128]{1,0:T(8,128)(2,1)} %param.13) | copy-start | bytes 3145732
  202.9 11.4 %copy-start.3 = (f32[64,4352]{1,0:T(8,128)S(1)}, f32[64,4352]{1,0:T(8,128)}, u32[]{:S(2)}) copy-start(f32[64,4352]{1,0:T(8,128)} %copy-done.2) | copy-start | bytes 3342340
  202.9 14.2 %copy-start.32 = (bf16[256,128]{1,0:T(8,128)(2,1)S(1)}, bf16[256,128]{1,0:T(8,128)(2,1)}, u32[]{:S(2)}) copy-start(bf16[256,128]{1,0:T(8,128)(2,1)} %get-tuple-element.44) | copy-start | bytes 196612
  202.9 24.4 %all-to-all-start.4 = ((bf16[16,8,2048]{2,1,0:T(8,128)(2,1)}), bf16[16,8,2048]{2,1,0:T(8,128)(2,1)S(1)}, u32[]{:S(2)}, u32[]{:S(2)}) async-start(bf16[16,8,2048]{2,1,0:T(8,128)(2,1)} %fusion.21), calls=%async_computation.4 | async-start | bytes 1048576 | tf_op jit(solution)/shard_map/all_to_all | solution.py:183
  212.9 5.4 %collective-permute-start.20 = (f32[256,384]{0,1:T(8,128)}, f32[256,384]{0,1:T(8,128)}, u32[]{:S(2)}, u32[]{:S(2)}) collective-permute-start(f32[256,384]{0,1:T(8,128)} %copy.85), channel_id=1, source_target_pairs={{0,1},{1,0},{2,3},{3,2},{4,5},{5,4},{6,7},{7,6},{8,9},{9,8},{10,11... | collective-permute-start | bytes 1179656 | tf_op jit(solution)/shard_map/ppermute | solution.py:59
  218.2 12.5 %copy-start.17 = (bf16[8,4096]{1,0:T(8,128)(2,1)S(1)}, bf16[8,4096]{1,0:T(8,128)(2,1)}, u32[]{:S(2)}) copy-start(bf16[8,4096]{1,0:T(8,128)(2,1)} %param.9) | copy-start | bytes 196612
  218.2 12.6 %copy-start.39 = (f32[8]{0:T(128)S(1)}, f32[8]{0:T(128)}, u32[]{:S(2)}) copy-start(f32[8]{0:T(128)} %copy-done.38) | copy-start | bytes 100
  218.2 12.6 %copy-start.41 = (f32[8]{0:T(128)S(1)}, f32[8]{0:T(128)}, u32[]{:S(2)}) copy-start(f32[8]{0:T(128)} %get-tuple-element.69) | copy-start | bytes 100
  227.4 3.2 %collective-permute-start.12 = (f32[8,2048]{1,0:T(8,128)S(1)}, f32[8,2048]{1,0:T(8,128)S(1)}, u32[]{:S(2)}, u32[]{:S(2)}) collective-permute-start(f32[8,2048]{1,0:T(8,128)S(1)} %convert_reduce_fusion.1), channel_id=1, source_target_pairs={{0,1},{1,0},{2,3},{3,2},{4,5},{5,4},{6,7},{7,6},{8,9},{9,8},{10,11... | collective-permute-start | bytes 196616 | tf_op jit(solution)/shard_map/ppermute | solution.py:59
  (7 other events, 7.7 us)
